TPU v7x, 256 devices: a whole 4x4x8 slice. The times are simulated.
256 devices in a mesh: gx: 8 (over y, core), gy: 8 (over x, z_hi), gz: 4 (over z_lo).
Axes of the slice: x: 4, y: 4, z: 8 (z_hi: 2, z_lo: 4; z = z_hi * 4 + z_lo), core: 2. Of those that a mesh axis runs over, the one named last changes fastest.
Arguments:
- pressure: float32 [256, 256, 512], P('gx', 'gy', 'gz'), may hold values from -6 to 6
- pressure_prev: float32 [256, 256, 512], P('gx', 'gy', 'gz'), may hold values from -6 to 6
- horiz_coef: float32 [256, 256, 512], P('gx', 'gy', 'gz'), may hold values from 0.04 to 0.19
- vert_coef: float32 [256, 256, 512], P('gx', 'gy', 'gz'), may hold values from 0.04 to 0.19
- traces: bfloat16 [256, 64, 2, 128], P(('gx', 'gy', 'gz')), may hold values from -6 to 6
- recv_cell: int32 [256, 64, 2], P(('gx', 'gy', 'gz')), may hold values from 0 to 131071, as said below
- recv_owner: int32 [256, 64, 2], P(('gx', 'gy', 'gz')), may hold values from 0 to 3, as said below
- trace_counts: int32 [256, 64], P(('gx', 'gy', 'gz')), may hold values from 0 to 2, as said below
Outputs:
- final_pressure: float32 [256, 256, 512], P('gx', 'gy', 'gz')
- final_prev: float32 [256, 256, 512], P('gx', 'gy', 'gz')
Inputs may be any that keep to these rules, and one draw needn't show every extreme that they name: `recv_cell`: flat index of a cell inside the 32 x 32 x 128 block of the owning subdomain, inline slowest. `recv_owner`: depth index of the owning subdomain within the destination column. `trace_counts`: slots at and past the count are unused; some column receives 2 slots from every holder in every draw.
All inputs are finite; a program needn't handle non-finite values.
Results may differ from a plain program's by a relative error of at most 0.00044.
Values may be sent and summed in bfloat16 or wider, within the bound.
A program may use at most 128 MiB of HBM per device.

v0:
```python
import jax
import jax.numpy as jnp
from jax import lax
from jax.sharding import PartitionSpec as P

STEPS = 32


COEF = (-205.0 / 72.0, 8.0 / 5.0, -1.0 / 5.0, 8.0 / 315.0, -1.0 / 560.0)


def with_halo(array, sides, width):
    for axis, dim in sides:
        devices, length = (lax.axis_size(axis), array.shape[dim])
        up = [(i, (i + 1) % devices) for i in range(devices - 1)]
        down = [(j, i) for i, j in up]
        last = lax.slice_in_dim(array, length - width, length, axis=dim)
        initial = lax.slice_in_dim(array, 0, width, axis=dim)
        before = lax.ppermute(last, axis, up)
        after = lax.ppermute(initial, axis, down)
        array = jnp.concatenate([before, array, after], axis=dim)
    return array


def laplace_terms(padded):
    sa, sb, sc = padded.shape
    na, nb, nc = (sa - 8, sb - 8, sc - 8)
    center = padded[4 : 4 + na, 4 : 4 + nb, 4 : 4 + nc]
    lxx = COEF[0] * center
    lyy = COEF[0] * center
    lzz = COEF[0] * center
    for k in range(1, 5):
        lxx = lxx + COEF[k] * (
            padded[4 + k : 4 + k + na, 4 : 4 + nb, 4 : 4 + nc]
            + padded[4 - k : 4 - k + na, 4 : 4 + nb, 4 : 4 + nc]
        )
        lyy = lyy + COEF[k] * (
            padded[4 : 4 + na, 4 + k : 4 + k + nb, 4 : 4 + nc]
            + padded[4 : 4 + na, 4 - k : 4 - k + nb, 4 : 4 + nc]
        )
        lzz = lzz + COEF[k] * (
            padded[4 : 4 + na, 4 : 4 + nb, 4 + k : 4 + k + nc]
            + padded[4 : 4 + na, 4 : 4 + nb, 4 - k : 4 - k + nc]
        )
    return (center, lxx + lyy, lzz)


def body(
    pressure, pressure_prev, horiz_coef, vert_coef, traces, recv_cell, recv_owner, trace_counts
):
    size_x, size_y, size_z = pressure.shape
    samples = traces.shape[-1]
    per_step = samples // STEPS
    box_table = (
        jnp.arange(samples, dtype=jnp.int32)[:, None] // per_step
        == STEPS - 1 - jnp.arange(STEPS, dtype=jnp.int32)[None, :]
    ).astype(jnp.bfloat16)
    routed = (
        lax.all_to_all(traces, ("gx", "gy"), split_axis=1, concat_axis=0, tiled=True),
        lax.all_to_all(recv_cell, ("gx", "gy"), split_axis=1, concat_axis=0, tiled=True),
        lax.all_to_all(recv_owner, ("gx", "gy"), split_axis=1, concat_axis=0, tiled=True),
        lax.all_to_all(trace_counts, ("gx", "gy"), split_axis=1, concat_axis=0, tiled=True),
    )
    loads, cells, owners, counts = (
        lax.all_gather(routed[0], "gz", axis=0, tiled=True),
        lax.all_gather(routed[1], "gz", axis=0, tiled=True),
        lax.all_gather(routed[2], "gz", axis=0, tiled=True),
        lax.all_gather(routed[3], "gz", axis=0, tiled=True),
    )
    flat = loads.reshape(-1, samples)
    amps = jnp.dot(flat, box_table, preferred_element_type=jnp.float32).astype(jnp.bfloat16)
    slots = jnp.arange(cells.shape[-1], dtype=jnp.int32)
    filled = (slots[None, None, :] < counts[:, :, None]).reshape(-1)
    flat_cells = cells.reshape(-1)
    flat_owners = owners.reshape(-1)
    live = filled & (flat_owners == lax.axis_index("gz"))
    plane_index = flat_cells // size_z
    depth_index = flat_cells % size_z
    plane_hot = (
        (plane_index[:, None] == jnp.arange(size_x * size_y, dtype=jnp.int32)[None, :])
        & live[:, None]
    ).astype(jnp.bfloat16)
    depth_hot = (depth_index[:, None] == jnp.arange(size_z, dtype=jnp.int32)[None, :]).astype(
        jnp.bfloat16
    )

    def source_field(step):
        amp_now = lax.dynamic_index_in_dim(amps, step, 1, keepdims=False)
        weighted = depth_hot * amp_now[:, None]
        placed = lax.dot_general(
            plane_hot, weighted, (((0,), (0,)), ((), ())), preferred_element_type=jnp.float32
        )
        return placed.reshape(size_x, size_y, size_z)

    def advance(step, carry):
        field, older = carry
        padded = with_halo(field, (("gx", 0), ("gy", 1), ("gz", 2)), 4)
        center, lhor, lver = laplace_terms(padded)
        fresh = 2.0 * center - older + horiz_coef * lhor + vert_coef * lver + source_field(step)
        return (fresh, field)

    final_pressure, final_prev = lax.fori_loop(0, STEPS, advance, (pressure, pressure_prev))
    return (final_pressure, final_prev)


def solution(mesh):
    placed = (
        P("gx", "gy", "gz"),
        P("gx", "gy", "gz"),
        P("gx", "gy", "gz"),
        P("gx", "gy", "gz"),
        P(("gx", "gy", "gz"), None, None, None),
        P(("gx", "gy", "gz"), None, None),
        P(("gx", "gy", "gz"), None, None),
        P(("gx", "gy", "gz"), None),
    )
    return jax.shard_map(
        body,
        mesh=mesh,
        in_specs=placed,
        out_specs=(P("gx", "gy", "gz"), P("gx", "gy", "gz")),
        check_vma=False,
    )
```

profile of v0, /device:TPU:1, one launch (start us, length us, event | category | flops | bytes accessed | tf_op | source)
XLA Modules:
  0.0 1439.7 jit_solution(11438266360929508899)
XLA Ops:
  3.3 15.6 %all-to-all-start.2 = ((s32[1,64,1]{2,0,1:T(1,128)}), s32[1,64,1]{2,0,1:T(1,128)S(1)}, u32[]{:S(2)}, u32[]{:S(2)}) async-start(s32[1,64,1]{2,0,1:T(1,128)} %copy.36), calls=%async_computation.2 | async-start | bytes 65536 | tf_op jit(solution)/shard_map/all_to_all | solution.py:62
  21.7 9.0 all-to-all-done.2
  36.9 5.9 all-reduce
  47.1 10.2 all-to-all-start.3
  57.2 11.3 all-gather.1
  70.2 14.7 %all-to-all-start = ((bf16[1,64,2,128]{3,2,0,1:T(2,128)(2,1)}), bf16[1,64,2,128]{3,2,0,1:T(2,128)(2,1)S(1)}, u32[]{:S(2)}, u32[]{:S(2)}) async-start(bf16[1,64,2,128]{3,2,0,1:T(2,128)(2,1)} %bitcast), calls=%async_computation | async-start | bytes 65536 | tf_op jit(solution)/shard_map/all_to_all | solution.py:59
  85.0 11.3 all-gather.3
  96.9 10.5 all-gather
  107.6 1331.3 %while.16 = (s32[]{:T(128)}, f32[32,32,128]{2,1,0:T(8,128)S(1)}, f32[32,32,128]{2,1,0:T(8,128)}, f32[32,32,128]{2,1,0:T(8,128)}, f32[32,32,128]{2,1,0:T(8,128)},...) while((s32[]{:T(128)}, f32[32,32,128]{2,1,0:T(8,128)S(1)}, ...), condition=%wide.region_1.2_spmd.clone, body=%wide.region_0.1_spmd.clone.sunk | while | flops 144545280 | bytes 33390536 | solution.py:102
  107.6 8.6 collective-permute-start
  121.9 6.8 collective-permute-start.2
  130.9 6.9 collective-permute-done.3
  166.8 5.5 collective-permute-start.2
  174.5 7.1 collective-permute-done.3
  186.6 5.5 collective-permute-start.5
  211.8 5.8 collective-permute-start.2
  219.0 7.8 collective-permute-done.3
  231.8 5.5 collective-permute-start.5
  246.6 5.6 collective-permute-start
  263.9 8.1 collective-permute-done.3
  277.1 7.1 collective-permute-start.5
  302.8 5.7 collective-permute-start.2
  310.4 7.4 collective-permute-done.3
  322.8 5.5 collective-permute-start.5
  352.1 7.8 collective-permute-done.3
  364.9 5.7 collective-permute-start.5
  389.1 5.9 collective-permute-start.2
  396.4 7.8 collective-permute-done.3
  439.7 7.9 collective-permute-done.3
  480.7 7.8 collective-permute-done.3
  493.6 5.5 collective-permute-start.5
  521.8 7.9 collective-permute-done.3
  534.8 5.4 collective-permute-start.5
  562.7 8.0 collective-permute-done.3
  603.3 7.9 collective-permute-done.3
  643.8 8.0 collective-permute-done.3
  656.9 5.3 collective-permute-start.5
  684.2 7.9 collective-permute-done.3
  724.7 8.0 collective-permute-done.3
  737.8 5.3 collective-permute-start.5
  765.0 7.9 collective-permute-done.3
  805.6 8.0 collective-permute-done.3
  818.6 5.3 collective-permute-start.5
  845.9 7.9 collective-permute-done.3
  886.5 8.0 collective-permute-done.3
  899.5 5.3 collective-permute-start.5
  926.8 7.9 collective-permute-done.3
  967.3 8.0 collective-permute-done.3
  980.4 5.3 collective-permute-start.5
  1007.7 7.9 collective-permute-done.3
  1048.2 8.0 collective-permute-done.3
  1061.3 5.3 collective-permute-start.5
  1088.5 7.9 collective-permute-done.3
  1129.1 8.0 collective-permute-done.3
  1142.1 5.3 collective-permute-start.5
  1169.4 7.9 collective-permute-done.3
  1209.9 8.0 collective-permute-done.3
  1223.0 5.3 collective-permute-start.5
  1250.3 7.9 collective-permute-done.3
  1290.8 8.0 collective-permute-done.3
  1303.9 5.3 collective-permute-start.5
  1331.2 7.9 collective-permute-done.3
  1371.7 8.0 collective-permute-done.3
  1412.0 7.9 collective-permute-done.3
  (1197 shorter events, 959.7 us)
Async XLA Ops:
  3.3 27.3 %all-to-all-start.2 = ((s32[1,64,1]{2,0,1:T(1,128)}), s32[1,64,1]{2,0,1:T(1,128)S(1)}, u32[]{:S(2)}, u32[]{:S(2)}) async-start(s32[1,64,1]{2,0,1:T(1,128)} %copy.36), calls=%async_computation.2 | async-start | bytes 65536 | tf_op jit(solution)/shard_map/all_to_all | solution.py:62
  30.6 16.4 %all-to-all-start.1 = ((s32[1,64,2]{2,0,1:T(1,128)}), s32[1,64,2]{2,0,1:T(1,128)S(1)}, u32[]{:S(2)}, u32[]{:S(2)}) async-start(s32[1,64,2]{2,0,1:T(1,128)} %copy.35), calls=%async_computation.1 | async-start | bytes 65536 | tf_op jit(solution)/shard_map/all_to_all | solution.py:60
  47.1 23.2 %all-to-all-start.3 = ((s32[1,64,2]{2,0,1:T(1,128)}), s32[1,64,2]{2,0,1:T(1,128)S(1)}, u32[]{:S(2)}, u32[]{:S(2)}) async-start(s32[1,64,2]{2,0,1:T(1,128)} %copy.37), calls=%async_computation.3 | async-start | bytes 65536 | tf_op jit(solution)/shard_map/all_to_all | solution.py:61
  70.2 26.7 %all-to-all-start = ((bf16[1,64,2,128]{3,2,0,1:T(2,128)(2,1)}), bf16[1,64,2,128]{3,2,0,1:T(2,128)(2,1)S(1)}, u32[]{:S(2)}, u32[]{:S(2)}) async-start(bf16[1,64,2,128]{3,2,0,1:T(2,128)(2,1)} %bitcast), calls=%async_computation | async-start | bytes 65536 | tf_op jit(solution)/shard_map/all_to_all | solution.py:59
  107.6 10.5 collective-permute-start
  121.9 9.0 collective-permute-start.2
  128.7 9.1 collective-permute-start.3
  140.5 8.7 collective-permute-start.4
  172.3 9.3 collective-permute-start.3
  184.3 9.6 collective-permute-start.4
  217.6 9.3 collective-permute-start.3
  229.5 9.5 collective-permute-start.4
  262.5 9.6 collective-permute-start.3
  274.8 11.2 collective-permute-start.4
  277.1 9.2 collective-permute-start.5
  308.5 9.3 collective-permute-start.3
  320.5 9.6 collective-permute-start.4
  350.6 9.3 collective-permute-start.3
  362.6 9.8 collective-permute-start.4
  395.0 9.3 collective-permute-start.3
  407.0 8.8 collective-permute-start.4
  438.2 9.4 collective-permute-start.3
  479.3 9.3 collective-permute-start.3
  491.3 9.6 collective-permute-start.4
  520.3 9.4 collective-permute-start.3
  532.5 9.5 collective-permute-start.4
  561.3 9.5 collective-permute-start.3
  573.5 8.7 collective-permute-start.4
  601.9 9.4 collective-permute-start.3
  642.4 9.5 collective-permute-start.3
  654.6 9.4 collective-permute-start.4
  682.7 9.4 collective-permute-start.3
  723.2 9.5 collective-permute-start.3
  735.5 9.4 collective-permute-start.4
  763.6 9.4 collective-permute-start.3
  775.7 8.7 collective-permute-start.4
  804.1 9.5 collective-permute-start.3
  816.3 9.4 collective-permute-start.4
  844.5 9.4 collective-permute-start.3
  856.6 8.7 collective-permute-start.4
  885.0 9.5 collective-permute-start.3
  897.2 9.4 collective-permute-start.4
  925.3 9.4 collective-permute-start.3
  965.9 9.5 collective-permute-start.3
  978.1 9.4 collective-permute-start.4
  1006.2 9.4 collective-permute-start.3
  1018.3 8.7 collective-permute-start.4
  1046.7 9.5 collective-permute-start.3
  1059.0 9.4 collective-permute-start.4
  1087.1 9.4 collective-permute-start.3
  1099.2 8.7 collective-permute-start.4
  1127.6 9.5 collective-permute-start.3
  1139.8 9.4 collective-permute-start.4
  1167.9 9.4 collective-permute-start.3
  1208.5 9.5 collective-permute-start.3
  1220.7 9.4 collective-permute-start.4
  1248.8 9.4 collective-permute-start.3
  1289.3 9.5 collective-permute-start.3
  1301.6 9.4 collective-permute-start.4
  1329.7 9.4 collective-permute-start.3
  1341.8 8.7 collective-permute-start.4
  1370.2 9.5 collective-permute-start.3
  1382.4 9.4 collective-permute-start.4
  1410.6 9.4 collective-permute-start.3
  (266 other events, 1214.3 us)
where the time goes:
time: 1450 us; the launch traced here: 1440 us
  starting transfers between devices  580 us (40%)
  waiting for transfers between devices  382 us (26%)
  local copies, waits for them, and re-layouts  269 us (19%)
  other arithmetic  138 us (10%)
  blocking collectives  39.1 us (3%)
  matrix products  24.6 us (2%)
    ppermute x96, starting transfers between devices, with_halo(): before = lax.ppermute(last, axis, up)  390 us
    ppermute x96, waiting for transfers between devices, with_halo(): after = lax.ppermute(initial, axis, down)  362 us
    ppermute x96, starting transfers between devices, with_halo(): after = lax.ppermute(initial, axis, down)  145 us
    slice x128, local copies, waits for them, and re-layouts, with_halo(): initial = lax.slice_in_dim(array, 0, width, axis=dim)  84.8 us
    concatenate x64, other arithmetic, with_halo(): array = jnp.concatenate([before, array, after], axis=dim)  69.2 us
    ppermute x32, local copies, waits for them, and re-layouts, with_halo(): before = lax.ppermute(last, axis, up)  68.2 us
    add x32, other arithmetic, advance(): 2.0 * center - older + horiz_coef * lhor + vert_coef * lver  66.4 us
    while x384, local copies, waits for them, and re-layouts  33.5 us
  transfers between devices with their start and end apart: 196, of which 98 were waited for; matrix products, arithmetic and copies ran while one was open for 8% of the time, Pallas kernels for 0%

commit v1 on v0

v1 whole, which is shorter than its diff:
```python
import functools

import jax
import jax.numpy as jnp
from jax import lax
from jax.experimental import pallas as pl
from jax.experimental.pallas import tpu as pltpu
from jax.sharding import PartitionSpec as P

STEPS = 32
MESH = pl.DeviceIdType.MESH
COEF = (-205.0 / 72.0, 8.0 / 5.0, -1.0 / 5.0, 8.0 / 315.0, -1.0 / 560.0)
SCALE = 5040.0
TAPS = (8064.0, -1008.0, 128.0, -9.0)

NY = 64
CHUNK = 16
NCH = NY // CHUNK
ROWS = CHUNK * 32
SLAB = 32
FIELD = (NY + 8) * SLAB
F32, BF16 = jnp.float32, jnp.bfloat16


def taps(distance):
    value = jnp.zeros(distance.shape, F32)
    for k in range(1, 5):
        value = jnp.where(distance == k, TAPS[k - 1], value)
    return value


def iota(shape, dim):
    return lax.broadcasted_iota(jnp.int32, shape, dim)


def kernel(
    p_ref, q_ref, h_ref, v_ref, f_ref, outp_ref, outq_ref,
    fld, hc, vc, kc, hl, hot, zhot, wgt, xs, xh, hb, zs, zh, place, raw, band, zout, zin,
    ysend, yrecv, xsend, xrecv, zsend, zrecv, psend, precv,
):
    gx, gy, gz = lax.axis_index("gx"), lax.axis_index("gy"), lax.axis_index("gz")
    nx, ny, nz = lax.axis_size("gx"), lax.axis_size("gy"), lax.axis_size("gz")
    half = lax.rem(gy, 2)
    partner = gy + 1 - 2 * half
    has = {
        ("x", 0): gx > 0, ("x", 1): gx < nx - 1,
        ("y", 0): gy > 1, ("y", 1): gy < ny - 2,
        ("z", 0): gz > 0, ("z", 1): gz < nz - 1,
    }
    peer = {
        ("x", 0): {"gx": gx - 1}, ("x", 1): {"gx": gx + 1},
        ("y", 0): {"gy": gy - 2}, ("y", 1): {"gy": gy + 2},
        ("z", 0): {"gz": gz - 1}, ("z", 1): {"gz": gz + 1},
    }

    def clear(ref, start, count):
        ref[pl.ds(start, count), :] = jnp.zeros((count, 128), F32)

    for par in range(2):
        clear(fld, par * FIELD, 4 * SLAB)
        clear(fld, par * FIELD + (NY + 4) * SLAB, 4 * SLAB)
    zh[...] = jnp.zeros_like(zh)

    barrier = pltpu.get_barrier_semaphore()
    pl.semaphore_signal(barrier, inc=1, device_id={"gy": partner}, device_id_type=MESH)
    greet = jnp.int32(1)
    for key, ok in has.items():

        @pl.when(ok)
        def _(key=key):
            pl.semaphore_signal(barrier, inc=1, device_id=peer[key], device_id_type=MESH)

        greet = greet + ok.astype(jnp.int32)
    pl.semaphore_wait(barrier, greet)

    def pair(n):
        return pltpu.make_async_remote_copy(
            src_ref=(p_ref, q_ref, h_ref, v_ref)[n],
            dst_ref=raw.at[n],
            send_sem=psend.at[n],
            recv_sem=precv.at[n],
            device_id={"gy": partner},
            device_id_type=MESH,
        )

    for n in range(4):
        pair(n).start()

    @pl.loop(0, NCH)
    def _(c):
        clear(hb, pl.multiple_of(c * ROWS, ROWS), ROWS)

    band[...] = taps(jnp.abs(lax.rem(iota((256, 128), 0), 128) - iota((256, 128), 1))).astype(BF16)
    row, depth = iota((16, 256), 0), lax.rem(iota((16, 256), 1), 128)
    m = lax.rem(row, 4)
    away = jnp.where(row < 8, 128 + m - depth, depth + 4 - m)
    upper = lax.rem(row, 8) >= 4
    value = taps(away)
    zout[0] = jnp.where(upper, 0.0, value).astype(BF16)
    zout[1] = jnp.where(upper, value, 0.0).astype(BF16)
    row, lane = lax.rem(iota((32, 128), 0), 16), iota((32, 128), 1)
    target = lax.rem(row, 4) + jnp.where(row >= 8, 124, 0)
    upper = lax.rem(row, 8) >= 4
    hit = lane == target
    zin[0] = jnp.where(hit & jnp.logical_not(upper), 1.0, 0.0).astype(BF16)
    zin[1] = jnp.where(hit & upper, 1.0, 0.0).astype(BF16)

    for col in range(2):
        packed = f_ref[col]
        for k in range(2):
            pick = iota((8, 128), 1) == 64 * k + 32 + iota((8, 128), 0)
            by_lane = lax.dot_general(
                jnp.where(pick, 1.0, 0.0).astype(BF16), packed,
                (((1,), (1,)), ((), ())), preferred_element_type=F32,
            )
            where = (by_lane[0:1] * 32.0 + by_lane[1:2]).astype(jnp.int32)
            mine = by_lane[3:4].astype(jnp.int32) == gz
            where = jnp.where(mine, where, -1)
            for block in range(4):
                at = iota((256, 256), 0) + block * 256
                hot[pl.ds(col * 1024 + block * 256, 256), pl.ds(k * 256, 256)] = jnp.where(
                    at == where, 1.0, 0.0
                ).astype(BF16)
            spread = jnp.where(iota((128, 128), 0) == 64 * k + 34, 1.0, 0.0).astype(BF16)
            z = jnp.dot(packed, spread, preferred_element_type=F32).astype(jnp.int32)
            zhot[pl.ds(col * 512 + k * 256, 256), :] = jnp.where(
                z == iota((256, 128), 1), 1.0, 0.0
            )

    def arrange(refs, first):
        @pl.loop(0, 32)
        def _(y):
            for j in range(4):
                take = pl.ds(j * 32 + y, 8, stride=128)
                put = pl.multiple_of((first + y) * SLAB + j * 8, 8)
                fld[pl.ds(put + 4 * SLAB, 8), :] = refs[0][take, :]
                fld[pl.ds(put + 4 * SLAB + FIELD, 8), :] = refs[1][take, :]
                h, v = refs[2][take, :], refs[3][take, :]
                hc[pl.ds(put, 8), :] = h
                vc[pl.ds(put, 8), :] = v * (1.0 / SCALE)
                kc[pl.ds(put, 8), :] = 2.0 + COEF[0] * (2.0 * h + v)

    arrange((p_ref, q_ref, h_ref, v_ref), 32 * half)
    for n in range(4):
        pair(n).wait_recv()
    arrange([raw.at[n] for n in range(4)], 32 - 32 * half)

    def y_copy(side, par):
        src = par * FIELD + (4 if side == 0 else NY) * SLAB
        dst = par * FIELD + (NY + 4 if side == 0 else 0) * SLAB
        return pltpu.make_async_remote_copy(
            src_ref=fld.at[pl.ds(pl.multiple_of(src, 128), 128)],
            dst_ref=fld.at[pl.ds(pl.multiple_of(dst, 128), 128)],
            send_sem=ysend.at[side],
            recv_sem=yrecv.at[1 - side, par],
            device_id=peer["y", side],
            device_id_type=MESH,
        )

    def y_wait(side, par):
        here = pl.ds(pl.multiple_of(par * FIELD + (0 if side == 0 else NY + 4) * SLAB, 128), 128)
        pltpu.make_async_remote_copy(
            src_ref=fld.at[here], dst_ref=fld.at[here], send_sem=ysend.at[side],
            recv_sem=yrecv.at[side, par], device_id=peer["y", side], device_id_type=MESH,
        ).wait_recv()

    def x_copy(side, c, par, there):
        rows = pl.ds(pl.multiple_of(c * CHUNK * 4, 64), CHUNK * 4)
        return pltpu.make_async_remote_copy(
            src_ref=xs.at[side, rows],
            dst_ref=xh.at[par, there, rows],
            send_sem=xsend.at[side, c],
            recv_sem=xrecv.at[there, par, c],
            device_id=peer["x", side],
            device_id_type=MESH,
        )

    def z_copy(side, c, par, there):
        return pltpu.make_async_remote_copy(
            src_ref=zs.at[c, pl.ds(8 - 8 * side, 8)],
            dst_ref=zh.at[par, c, pl.ds(8 * there, 8)],
            send_sem=zsend.at[side, c],
            recv_sem=zrecv.at[there, par, c],
            device_id=peer["z", side],
            device_id_type=MESH,
        )

    def settle(c):
        for side in range(2):

            @pl.when(has["x", side])
            def _():
                x_copy(side, c, 0, 1 - side).wait_send()

            @pl.when(has["z", side])
            def _():
                z_copy(side, c, 0, 1 - side).wait_send()

            @pl.when(has["y", side] & (c == (0 if side == 0 else NCH - 1)))
            def _():
                y_copy(side, 0).wait_send()

    def send(c, par):
        for side in range(2):

            @pl.when(has["y", side] & (c == (0 if side == 0 else NCH - 1)))
            def _():
                y_copy(side, par).start()

        first = par * FIELD + (4 + c * CHUNK) * SLAB
        rows = pl.ds(pl.multiple_of(c * CHUNK * 4, 64), CHUNK * 4)
        for side in range(2):
            xs[side, rows, :] = fld[pl.ds(first + 7 * side, CHUNK * 4, stride=8), :]

            @pl.when(has["x", side])
            def _():
                x_copy(side, c, par, 1 - side).start()

        start = pl.multiple_of(c * ROWS, ROWS)
        dims = (((1,), (1,)), ((), ()))
        zs[c] = lax.dot_general(
            zout[0], hl[pl.ds(start, 256), :], dims, preferred_element_type=F32
        ) + lax.dot_general(
            zout[1], hl[pl.ds(start + 256, 256), :], dims, preferred_element_type=F32
        )
        for side in range(2):

            @pl.when(has["z", side])
            def _():
                z_copy(side, c, par, 1 - side).start()

    def split(start, new):
        high = new.astype(BF16)
        hl[pl.ds(start, SLAB), 0:128] = high
        hl[pl.ds(start, SLAB), 128:256] = (new - high.astype(F32)).astype(BF16)

    @pl.loop(0, NCH)
    def _(i):
        c = jnp.where(i == 0, 0, jnp.where(i == 1, NCH - 1, i - 1))

        @pl.loop(0, CHUNK)
        def _(y):
            start = pl.multiple_of(c * ROWS + y * SLAB, SLAB)
            split(start, fld[pl.ds(start + 4 * SLAB, SLAB), :])

        send(c, 0)

    sub = iota((8, 128), 0)

    def step(t, carry):
        par = lax.rem(t, 2)
        old, now = (1 - par) * FIELD + 4 * SLAB, par * FIELD + 4 * SLAB

        for col in range(2):
            for k in range(2):
                spread = jnp.where(iota((128, 128), 0) == 64 * k + t, 1.0, 0.0).astype(BF16)
                amp = jnp.dot(f_ref[col], spread, preferred_element_type=F32)
                at = pl.ds(col * 512 + k * 256, 256)
                wgt[at, :] = (zhot[at, :] * amp).astype(BF16)

        @pl.loop(0, 2 * NCH)
        def _(b):
            r = pl.multiple_of(b * 256, 256)
            col = pl.multiple_of((b // NCH) * 512, 512)
            rows = pl.ds(r, 256)
            inner = jnp.dot(hl[rows, :], band[...], preferred_element_type=F32)
            source = jnp.dot(hot[rows, :], wgt[pl.ds(col, 512), :], preferred_element_type=F32)
            was = pl.ds(pl.multiple_of(old + r, 128), 256)
            fld[was, :] = (
                source
                - fld[was, :]
                + kc[rows, :] * fld[pl.ds(pl.multiple_of(now + r, 128), 256), :]
                + vc[rows, :] * inner
            )

        @pl.loop(0, NCH)
        def _(i):
            c = jnp.where(i == 0, 0, jnp.where(i == 1, NCH - 1, i - 1))
            first = pl.multiple_of(c * ROWS, ROWS)
            for side in range(2):

                @pl.when(has["y", side] & (c == (0 if side == 0 else NCH - 1)))
                def _():
                    y_wait(side, par)

                @pl.when(has["x", side])
                def _():
                    x_copy(side, c, par, side).wait_recv()
                    rows = pl.ds(pl.multiple_of(c * CHUNK * 4, 64), CHUNK * 4)
                    hb[pl.ds(first + 7 * side, CHUNK * 4, stride=8), :] = xh[par, side, rows, :]

                @pl.when(has["z", side])
                def _():
                    z_copy(side, c, par, side).wait_recv()

            got = zh[par, c]
            high = got.astype(BF16)
            both = jnp.concatenate([high, (got - high.astype(F32)).astype(BF16)], axis=0)
            for n in range(2):
                place[pl.ds(256 * n, 256), :] = lax.dot_general(
                    both, zin[n], (((0,), (0,)), ((), ())), preferred_element_type=F32
                )
            settle(c)

            @pl.loop(0, CHUNK)
            def _(y):
                at = pl.multiple_of(y * SLAB, SLAB)
                r = pl.multiple_of(first + y * SLAB, SLAB)
                base = pl.multiple_of(now + r, SLAB)
                mid = [fld[pl.ds(base + 8 * j, 8), :] for j in range(4)]
                edge = [hb[pl.ds(r + 8 * j, 8), :] for j in range(4)]
                below = [jnp.where(sub == 0, e, pltpu.roll(v, 1, 0)) for e, v in zip(edge, mid)]
                above = [jnp.where(sub == 7, e, pltpu.roll(v, 7, 0)) for e, v in zip(edge, mid)]
                line = below + mid + above
                tiles = []
                for j in range(4):
                    total = None
                    for k in range(1, 5):
                        near = (line[4 + j + k] + line[4 + j - k]) + (
                            fld[pl.ds(base + 8 * j + k * SLAB, 8), :]
                            + fld[pl.ds(base + 8 * j - k * SLAB, 8), :]
                        )
                        near = COEF[k] * near
                        total = near if total is None else total + near
                    here = pl.ds(r + 8 * j, 8)
                    was = pl.ds(pl.multiple_of(old + r, SLAB) + 8 * j, 8)
                    new = (
                        fld[was, :]
                        + hc[here, :] * total
                        + vc[here, :] * place[pl.ds(at + 8 * j, 8), :]
                    )
                    fld[was, :] = new
                    tiles.append(new)
                split(r, jnp.concatenate(tiles, axis=0))

            @pl.when(t < STEPS - 1)
            def _():
                send(c, 1 - par)

        return carry

    lax.fori_loop(0, STEPS, step, 0)
    for n in range(4):
        pair(n).wait_send()

    @pl.loop(0, 32)
    def _(y):
        for j in range(4):
            put = pl.ds(j * 32 + y, 8, stride=128)
            take = pl.multiple_of((4 + 32 * half + y) * SLAB + j * 8, 8)
            outp_ref[put, :] = fld[pl.ds(take, 8), :]
            outq_ref[put, :] = fld[pl.ds(take + FIELD, 8), :]


def body(
    pressure, pressure_prev, horiz_coef, vert_coef, traces, recv_cell, recv_owner, trace_counts
):
    samples = traces.shape[-1]
    columns, slots = recv_cell.shape[1:]
    per_step = samples // STEPS
    box_table = (
        jnp.arange(samples, dtype=jnp.int32)[:, None] // per_step
        == STEPS - 1 - jnp.arange(STEPS, dtype=jnp.int32)[None, :]
    ).astype(BF16)
    amps = jnp.dot(
        traces.reshape(-1, samples), box_table, preferred_element_type=F32
    ).astype(BF16).reshape(columns, slots, STEPS)
    cell = recv_cell[0]
    x, y, z = cell // 4096, (cell // 128) % 32, cell % 128
    live = jnp.arange(slots, dtype=jnp.int32)[None, :] < trace_counts[0][:, None]
    owner = jnp.where(live, recv_owner[0], -1)
    code = jnp.stack([y, (x % 4) * 8 + x // 4, z, owner], axis=-1).astype(BF16)
    packed = jnp.concatenate(
        [amps, code, jnp.zeros((columns, slots, 28), BF16)], axis=-1
    ).reshape(columns, 128)
    routed = lax.all_to_all(packed, ("gx", "gy"), split_axis=0, concat_axis=0, tiled=True)
    own = lax.all_gather(routed, "gz", axis=0, tiled=True)
    pairs = [(i, i ^ 1) for i in range(lax.axis_size("gy"))]
    other = lax.ppermute(own, "gy", pairs)
    low = lax.rem(lax.axis_index("gy"), 2) == 0
    table = jnp.stack([jnp.where(low, own, other), jnp.where(low, other, own)])

    flat = [a.reshape(1024, 128) for a in (pressure, pressure_prev, horiz_coef, vert_coef)]
    vmem = pl.BlockSpec(memory_space=pltpu.VMEM)
    dma = pltpu.SemaphoreType.DMA
    outs = pl.pallas_call(
        kernel,
        out_shape=[jax.ShapeDtypeStruct((1024, 128), F32)] * 2,
        in_specs=[vmem] * 5,
        out_specs=[vmem] * 2,
        scratch_shapes=[
            pltpu.VMEM((2 * FIELD, 128), F32),
            pltpu.VMEM((NY * SLAB, 128), F32),
            pltpu.VMEM((NY * SLAB, 128), F32),
            pltpu.VMEM((NY * SLAB, 128), F32),
            pltpu.VMEM((NY * SLAB, 256), BF16),
            pltpu.VMEM((NY * SLAB, 512), BF16),
            pltpu.VMEM((1024, 128), F32),
            pltpu.VMEM((1024, 128), BF16),
            pltpu.VMEM((2, NY * 4, 128), F32),
            pltpu.VMEM((2, 2, NY * 4, 128), F32),
            pltpu.VMEM((NY * SLAB, 128), F32),
            pltpu.VMEM((NCH, 16, 256), F32),
            pltpu.VMEM((2, NCH, 16, 256), F32),
            pltpu.VMEM((ROWS, 128), F32),
            pltpu.VMEM((4, 1024, 128), F32),
            pltpu.VMEM((256, 128), BF16),
            pltpu.VMEM((2, 16, 256), BF16),
            pltpu.VMEM((2, 32, 128), BF16),
            dma((2,)), dma((2, 2)),
            dma((2, NCH)), dma((2, 2, NCH)),
            dma((2, NCH)), dma((2, 2, NCH)),
            dma((4,)), dma((4,)),
        ],
        compiler_params=pltpu.CompilerParams(
            collective_id=0, has_side_effects=True, vmem_limit_bytes=40 * 1024 * 1024
        ),
    )(*flat, table)
    return tuple(o.reshape(32, 32, 128) for o in outs)


def solution(mesh):
    block = P("gx", "gy", "gz")
    placed = (
        block,
        block,
        block,
        block,
        P(("gx", "gy", "gz"), None, None, None),
        P(("gx", "gy", "gz"), None, None),
        P(("gx", "gy", "gz"), None, None),
        P(("gx", "gy", "gz"), None),
    )
    return jax.shard_map(
        body, mesh=mesh, in_specs=placed, out_specs=(block, block), check_vma=False
    )
```

time: 1450 us -> 404 us (0.28)
  starting transfers between devices: 580 us -> 0.26 us
  waiting for transfers between devices: 382 us -> 6.76 us
  Pallas kernels: 0 us -> 350 us
  local copies, waits for them, and re-layouts: 269 us -> 4.7 us
  other arithmetic: 138 us -> 0.83 us
  matrix products: 24.6 us -> 0.24 us
    ppermute x192 -> x1, starting transfers between devices: 535 us -> 0.26 us  [body(): other = lax.ppermute(own, 'gy', pairs)]
    ppermute x192 -> x1, waiting for transfers between devices: 369 us -> 6.76 us  [body(): other = lax.ppermute(own, 'gy', pairs)]
    pallas_call x0 -> x1, Pallas kernels: none -> 350 us  [body(): pl.pallas_call(kernel, out_shape=[jax.ShapeDtypeStruct((1024, 128), F32)]...]
    slice x160 -> x0, local copies, waits for them, and re-layouts: 116 us -> none  [the longest x128 84.8 us: with_halo(): initial = lax.slice_in_dim(array, 0, width, axis=dim)]
    ppermute x64 -> x0, local copies, waits for them, and re-layouts: 79.7 us -> none  [the longest x32 68.2 us: with_halo(): before = lax.ppermute(last, axis, up)]
    concatenate x64 -> x0, other arithmetic: 69.2 us -> none  [with_halo(): array = jnp.concatenate([before, array, after], axis=dim)]
    add x32 -> x0, other arithmetic: 66.4 us -> none  [advance(): 2.0 * center - older + horiz_coef * lhor + vert_coef * lver]
    all_to_all x4 -> x0, starting transfers between devices: 45.2 us -> none  [the longest x1 15.6 us: body(): lax.all_to_all(trace_counts, ('gx', 'gy'), split_axis=1, concat_axis=0, t...]
  transfers between devices with their start and end apart: 196 -> 1, of which waited for: 98 -> 1; matrix products, arithmetic and copies ran while one was open for 8% -> 0% of each run, Pallas kernels for 0% -> 0%
where the time goes in v1:
time: 404 us; the launch traced here: 401 us
  Pallas kernels  350 us (87%)
  blocking collectives  37.3 us (9%)
  waiting for transfers between devices  6.76 us (2%)
  local copies, waits for them, and re-layouts  4.7 us (1%)
    pallas_call x1, Pallas kernels, body(): pl.pallas_call(kernel, out_shape=[jax.ShapeDtypeStruct((1024, 128), F32)]...  350 us
    all_to_all x1, blocking collectives, body(): lax.all_to_all(packed, ('gx', 'gy'), split_axis=0, concat_axis=0, tiled=T...  27.1 us
    all_gather x1, blocking collectives, body(): own = lax.all_gather(routed, 'gz', axis=0, tiled=True)  10.2 us
  transfers between devices with their start and end apart: 1, of which 1 were waited for; matrix products, arithmetic and copies ran while one was open for 0% of the time, Pallas kernels for 0%

profile of v1, /device:TPU:1, one launch (start us, length us, event | category | flops | bytes accessed | tf_op | source)
XLA Modules:
  0.0 401.3 jit_solution(7682214028159628131)
XLA Ops:
  0.6 0.0 copy-start
  0.7 0.0 copy-start.7
  0.7 0.7 copy-done
  1.4 0.0 copy-start.5
  1.4 0.0 copy-start.6
  1.4 0.0 copy-start.3
  1.4 0.2 fusion
  1.6 0.1 copy.21
  1.8 0.3 copy-done.5
  2.1 0.1 copy.22
  2.2 0.0 copy-done.6
  2.2 0.1 copy.26
  2.3 0.0 copy-done.7
  2.3 0.8 fusion.5
  3.2 0.0 copy-start.1
  3.2 0.0 copy-start.2
  3.2 0.5 concatenate.4
  3.7 0.1 all_to_all.11
  3.8 27.1 %all_to_all.13 = bf16[64,1,128]{2,1,0:T(2,128)(2,1)S(1)} all-to-all(bf16[64,1,128]{2,1,0:T(2,128)(2,1)S(1)} %all_to_all.11), channel_id=1, replica_groups=mesh['gx'=8,'gy'=8,'gz'=4] {'gx','gy'}, dimensions={0} | all-to-all | bytes 32768 | tf_op jit(solution)/shard_map/all_to_all | solution.py:376
  30.9 10.2 %all-gather = bf16[256,1,128]{2,0,1:T(8,128)(2,1)S(1)} all-gather(bf16[64,1,128]{2,0,1:T(8,128)(2,1)S(1)} %copy.28), channel_id=2, replica_groups=mesh['gx'=8,'gy'=8,'gz'=4] {'gz'}, dimensions={0}, use_global_device_ids=true | all-gather | bytes 81920 | tf_op jit(solution)/shard_map/all_gather | solution.py:377
  41.2 0.3 collective-permute-start
  41.4 6.8 %collective-permute-done = bf16[256,128]{1,0:T(8,128)(2,1)S(1)} collective-permute-done((bf16[256,128]{1,0:T(8,128)(2,1)S(1)}, bf16[256,128]{1,0:T(8,128)(2,1)S(1)}, u32[]{:S(2)}, u32[]{:S(2)}) %collective-permute-start) | collective-permute-done | bytes 65568 | tf_op jit(solution)/shard_map/ppermute | solution.py:379
  48.2 0.0 copy-done.3
  48.2 0.0 copy-done.1
  48.3 0.0 copy-done.2
  48.3 0.0 copy-start.4
  48.3 1.0 copy-done.4
  49.3 350.4 %shard_map.95 = (f32[1024,128]{1,0:T(8,128)S(1)}, f32[1024,128]{1,0:T(8,128)S(1)}) custom-call(f32[1024,128]{1,0:T(8,128)S(1)} %bitcast.22, f32[1024,128]{1,0:T(8,128)S(1)} %bitcast.23, f32[1024,128]{1,0:T(8,128)S(1)} %bitcast.24, f32[1024,128]{1,0:T(8,128)S(1)} %bitcast.25, bf16[2,256,128]{2,1,0:T(8,128)(2,1)S(1)} %pad_maximum_fusion.f_ref), custom_call_target="tpu_custom_call" | custom-call | tf_op jit(solution)/shard_map/pallas_call | solution.py:386
  399.7 0.8 copy.31
  400.5 0.8 copy.32
  (6 shorter events, 0.1 us)
Async XLA Ops:
  0.6 0.8 copy-start
  0.7 1.7 copy-start.7
  1.4 0.7 copy-start.5
  1.4 0.8 copy-start.6
  1.4 46.8 %copy-start.3 = (f32[32,32,128]{2,1,0:T(8,128)S(1)}, f32[32,32,128]{2,1,0:T(8,128)}, u32[]{:S(2)}) copy-start(f32[32,32,128]{2,1,0:T(8,128)} %param.10) | copy-start | bytes 1572868
  3.2 45.1 %copy-start.1 = (f32[32,32,128]{2,1,0:T(8,128)S(1)}, f32[32,32,128]{2,1,0:T(8,128)}, u32[]{:S(2)}) copy-start(f32[32,32,128]{2,1,0:T(8,128)} %param.8) | copy-start | bytes 1572868
  3.2 45.1 %copy-start.2 = (f32[32,32,128]{2,1,0:T(8,128)S(1)}, f32[32,32,128]{2,1,0:T(8,128)}, u32[]{:S(2)}) copy-start(f32[32,32,128]{2,1,0:T(8,128)} %param.9) | copy-start | bytes 1572868
  41.2 7.0 %collective-permute-start = (bf16[256,128]{1,0:T(8,128)(2,1)S(1)}, bf16[256,128]{1,0:T(8,128)(2,1)S(1)}, u32[]{:S(2)}, u32[]{:S(2)}) collective-permute-start(bf16[256,128]{1,0:T(8,128)(2,1)S(1)} %bitcast.28), channel_id=1, source_target_pairs={{0,4},{4,0},{8,12},{12,8},{16,20},{20,16},{24,28},{28,24},{1,5},{5... | collective-permute-start | bytes 196616 | tf_op jit(solution)/shard_map/ppermute | solution.py:379
  48.3 1.0 copy-start.4

commit v2 on v1

--- a/solution.py
+++ b/solution.py
@@ -17,6 +17,7 @@
 CHUNK = 16
 NCH = NY // CHUNK
 ROWS = CHUNK * 32
+GROUP = 4
 SLAB = 32
 FIELD = (NY + 8) * SLAB
 F32, BF16 = jnp.float32, jnp.bfloat16
@@ -29,19 +30,26 @@
     return value
 
 
+def code(value):
+    return jnp.round((value - 0.115) * (32767.0 / 0.075)).astype(jnp.int16)
+
+
+def decode(value):
+    return value.astype(jnp.int32).astype(F32) * (0.075 / 32767.0) + 0.115
+
+
 def iota(shape, dim):
     return lax.broadcasted_iota(jnp.int32, shape, dim)
 
 
 def kernel(
-    p_ref, q_ref, h_ref, v_ref, f_ref, outp_ref, outq_ref,
-    fld, hc, vc, kc, hl, hot, zhot, wgt, xs, xh, hb, zs, zh, place, raw, band, zout, zin,
-    ysend, yrecv, xsend, xrecv, zsend, zrecv, psend, precv,
+    p_ref, q_ref, h_ref, v_ref, op_ref, oq_ref, oh_ref, ov_ref, f_ref, outp_ref, outq_ref,
+    fld, hc, vc, kc, hl, hot, zhot, wgt, xs, xh, hb, zs, zh, raw, band, lap, src,
+    ysend, yrecv, xsend, xrecv, zsend, zrecv,
 ):
     gx, gy, gz = lax.axis_index("gx"), lax.axis_index("gy"), lax.axis_index("gz")
     nx, ny, nz = lax.axis_size("gx"), lax.axis_size("gy"), lax.axis_size("gz")
     half = lax.rem(gy, 2)
-    partner = gy + 1 - 2 * half
     has = {
         ("x", 0): gx > 0, ("x", 1): gx < nx - 1,
         ("y", 0): gy > 1, ("y", 1): gy < ny - 2,
@@ -62,8 +70,7 @@
     zh[...] = jnp.zeros_like(zh)
 
     barrier = pltpu.get_barrier_semaphore()
-    pl.semaphore_signal(barrier, inc=1, device_id={"gy": partner}, device_id_type=MESH)
-    greet = jnp.int32(1)
+    greet = jnp.int32(0)
     for key, ok in has.items():
 
         @pl.when(ok)
@@ -73,37 +80,14 @@
         greet = greet + ok.astype(jnp.int32)
     pl.semaphore_wait(barrier, greet)
 
-    def pair(n):
-        return pltpu.make_async_remote_copy(
-            src_ref=(p_ref, q_ref, h_ref, v_ref)[n],
-            dst_ref=raw.at[n],
-            send_sem=psend.at[n],
-            recv_sem=precv.at[n],
-            device_id={"gy": partner},
-            device_id_type=MESH,
-        )
-
-    for n in range(4):
-        pair(n).start()
-
     @pl.loop(0, NCH)
     def _(c):
         clear(hb, pl.multiple_of(c * ROWS, ROWS), ROWS)
 
-    band[...] = taps(jnp.abs(lax.rem(iota((256, 128), 0), 128) - iota((256, 128), 1))).astype(BF16)
-    row, depth = iota((16, 256), 0), lax.rem(iota((16, 256), 1), 128)
-    m = lax.rem(row, 4)
-    away = jnp.where(row < 8, 128 + m - depth, depth + 4 - m)
-    upper = lax.rem(row, 8) >= 4
-    value = taps(away)
-    zout[0] = jnp.where(upper, 0.0, value).astype(BF16)
-    zout[1] = jnp.where(upper, value, 0.0).astype(BF16)
-    row, lane = lax.rem(iota((32, 128), 0), 16), iota((32, 128), 1)
-    target = lax.rem(row, 4) + jnp.where(row >= 8, 124, 0)
-    upper = lax.rem(row, 8) >= 4
-    hit = lane == target
-    zin[0] = jnp.where(hit & jnp.logical_not(upper), 1.0, 0.0).astype(BF16)
-    zin[1] = jnp.where(hit & upper, 1.0, 0.0).astype(BF16)
+    depth = lax.rem(iota((256, 128), 0), 128)
+    band[:, 0:128] = taps(jnp.abs(depth - iota((256, 128), 1))).astype(BF16)
+    m = lax.rem(iota((256, 128), 1), 8)
+    band[:, 128:256] = taps(jnp.where(m < 4, 128 + m - depth, depth + 8 - m)).astype(BF16)
 
     for col in range(2):
         packed = f_ref[col]
@@ -141,9 +125,14 @@
                 kc[pl.ds(put, 8), :] = 2.0 + COEF[0] * (2.0 * h + v)
 
     arrange((p_ref, q_ref, h_ref, v_ref), 32 * half)
-    for n in range(4):
-        pair(n).wait_recv()
-    arrange([raw.at[n] for n in range(4)], 32 - 32 * half)
+    raw[0] = decode(oh_ref[...])
+    raw[1] = decode(ov_ref[...])
+    arrange((op_ref, oq_ref, raw.at[0], raw.at[1]), 32 - 32 * half)
+
+    sub, lane = iota((8, 128), 0), iota((8, 128), 1)
+    group = lax.rem((lane + 4) // 8, 16)
+    rim = (lane < 4) | (lane >= 124)
+    lower = lax.rem(lane, 8) < 4
 
     def y_copy(side, par):
         src = par * FIELD + (4 if side == 0 else NY) * SLAB
@@ -177,8 +166,8 @@
 
     def z_copy(side, c, par, there):
         return pltpu.make_async_remote_copy(
-            src_ref=zs.at[c, pl.ds(8 - 8 * side, 8)],
-            dst_ref=zh.at[par, c, pl.ds(8 * there, 8)],
+            src_ref=zs.at[c],
+            dst_ref=zh.at[par, c, there],
             send_sem=zsend.at[side, c],
             recv_sem=zrecv.at[there, par, c],
             device_id=peer["z", side],
@@ -217,12 +206,14 @@
                 x_copy(side, c, par, 1 - side).start()
 
         start = pl.multiple_of(c * ROWS, ROWS)
-        dims = (((1,), (1,)), ((), ()))
-        zs[c] = lax.dot_general(
-            zout[0], hl[pl.ds(start, 256), :], dims, preferred_element_type=F32
-        ) + lax.dot_general(
-            zout[1], hl[pl.ds(start + 256, 256), :], dims, preferred_element_type=F32
-        )
+        both = jnp.dot(hl[pl.ds(start, ROWS), :], band[...], preferred_element_type=F32)
+        lap[pl.ds(start, ROWS), :] = both[:, 0:128]
+        for n in range(4):
+            packed = both[128 * n : 128 * n + 8, 128:256]
+            for i in range(1, 16):
+                at = 128 * n + 8 * i
+                packed = jnp.where(group == i, both[at : at + 8, 128:256], packed)
+            zs[c, pl.ds(8 * n, 8), :] = packed
         for side in range(2):
 
             @pl.when(has["z", side])
@@ -245,33 +236,30 @@
 
         send(c, 0)
 
-    sub = iota((8, 128), 0)
-
     def step(t, carry):
         par = lax.rem(t, 2)
         old, now = (1 - par) * FIELD + 4 * SLAB, par * FIELD + 4 * SLAB
 
-        for col in range(2):
-            for k in range(2):
-                spread = jnp.where(iota((128, 128), 0) == 64 * k + t, 1.0, 0.0).astype(BF16)
-                amp = jnp.dot(f_ref[col], spread, preferred_element_type=F32)
-                at = pl.ds(col * 512 + k * 256, 256)
-                wgt[at, :] = (zhot[at, :] * amp).astype(BF16)
-
-        @pl.loop(0, 2 * NCH)
-        def _(b):
-            r = pl.multiple_of(b * 256, 256)
-            col = pl.multiple_of((b // NCH) * 512, 512)
-            rows = pl.ds(r, 256)
-            inner = jnp.dot(hl[rows, :], band[...], preferred_element_type=F32)
-            source = jnp.dot(hot[rows, :], wgt[pl.ds(col, 512), :], preferred_element_type=F32)
-            was = pl.ds(pl.multiple_of(old + r, 128), 256)
-            fld[was, :] = (
-                source
-                - fld[was, :]
-                + kc[rows, :] * fld[pl.ds(pl.multiple_of(now + r, 128), 256), :]
-                + vc[rows, :] * inner
-            )
+        @pl.when(par == 0)
+        def _():
+            for col in range(2):
+                for k in range(2):
+                    when = 64 * k + t + iota((128, 256), 1) // 128
+                    spread = jnp.where(iota((128, 256), 0) == when, 1.0, 0.0).astype(BF16)
+                    amp = jnp.dot(f_ref[col], spread, preferred_element_type=F32)
+                    at = pl.ds(col * 512 + k * 256, 256)
+                    wgt[at, 0:128] = (zhot[at, :] * amp[:, 0:128]).astype(BF16)
+                    wgt[at, 128:256] = (zhot[at, :] * amp[:, 128:256]).astype(BF16)
+
+            @pl.loop(0, 2 * NCH)
+            def _(b):
+                rows = pl.ds(pl.multiple_of(b * 256, 256), 256)
+                col = pl.multiple_of((b // NCH) * 512, 512)
+                both = jnp.dot(
+                    hot[rows, :], wgt[pl.ds(col, 512), :], preferred_element_type=F32
+                )
+                src[0, rows, :] = both[:, 0:128]
+                src[1, rows, :] = both[:, 128:256]
 
         @pl.loop(0, NCH)
         def _(i):
@@ -293,45 +281,48 @@
                 def _():
                     z_copy(side, c, par, side).wait_recv()
 
-            got = zh[par, c]
-            high = got.astype(BF16)
-            both = jnp.concatenate([high, (got - high.astype(F32)).astype(BF16)], axis=0)
-            for n in range(2):
-                place[pl.ds(256 * n, 256), :] = lax.dot_general(
-                    both, zin[n], (((0,), (0,)), ((), ())), preferred_element_type=F32
-                )
             settle(c)
 
-            @pl.loop(0, CHUNK)
+            @pl.loop(0, CHUNK // GROUP)
             def _(y):
-                at = pl.multiple_of(y * SLAB, SLAB)
-                r = pl.multiple_of(first + y * SLAB, SLAB)
+                at = pl.multiple_of(y * (GROUP * SLAB), GROUP * SLAB)
+                r = pl.multiple_of(first + at, GROUP * SLAB)
                 base = pl.multiple_of(now + r, SLAB)
-                mid = [fld[pl.ds(base + 8 * j, 8), :] for j in range(4)]
-                edge = [hb[pl.ds(r + 8 * j, 8), :] for j in range(4)]
-                below = [jnp.where(sub == 0, e, pltpu.roll(v, 1, 0)) for e, v in zip(edge, mid)]
-                above = [jnp.where(sub == 7, e, pltpu.roll(v, 7, 0)) for e, v in zip(edge, mid)]
-                line = below + mid + above
-                tiles = []
-                for j in range(4):
-                    total = None
-                    for k in range(1, 5):
-                        near = (line[4 + j + k] + line[4 + j - k]) + (
-                            fld[pl.ds(base + 8 * j + k * SLAB, 8), :]
-                            + fld[pl.ds(base + 8 * j - k * SLAB, 8), :]
+                back = pl.multiple_of(old + r, SLAB)
+                mine = pl.ds(pl.multiple_of(y * 8, 8), 8)
+                got = jnp.where(lower, zh[par, c, 0, mine, :], zh[par, c, 1, mine, :])
+                fresh = []
+                for g in range(GROUP):
+                    mid = [fld[pl.ds(base + SLAB * g + 8 * j, 8), :] for j in range(4)]
+                    edge = [hb[pl.ds(r + SLAB * g + 8 * j, 8), :] for j in range(4)]
+                    below = [jnp.where(sub == 0, e, pltpu.roll(v, 1, 0)) for e, v in zip(edge, mid)]
+                    above = [jnp.where(sub == 7, e, pltpu.roll(v, 7, 0)) for e, v in zip(edge, mid)]
+                    line = below + mid + above
+                    tiles = []
+                    for j in range(4):
+                        spot = SLAB * g + 8 * j
+                        total = None
+                        for k in range(1, 5):
+                            near = (line[4 + j + k] + line[4 + j - k]) + (
+                                fld[pl.ds(base + spot + k * SLAB, 8), :]
+                                + fld[pl.ds(base + spot - k * SLAB, 8), :]
+                            )
+                            near = COEF[k] * near
+                            total = near if total is None else total + near
+                        here = pl.ds(r + spot, 8)
+                        turn = (128 - spot) % 128
+                        rolled = pltpu.roll(got, turn, 1) if turn else got
+                        depth = lap[here, :] + jnp.where(rim, rolled, 0.0)
+                        tiles.append(
+                            (src[par, here, :] - fld[pl.ds(back + spot, 8), :])
+                            + kc[here, :] * mid[j]
+                            + hc[here, :] * total
+                            + vc[here, :] * depth
                         )
-                        near = COEF[k] * near
-                        total = near if total is None else total + near
-                    here = pl.ds(r + 8 * j, 8)
-                    was = pl.ds(pl.multiple_of(old + r, SLAB) + 8 * j, 8)
-                    new = (
-                        fld[was, :]
-                        + hc[here, :] * total
-                        + vc[here, :] * place[pl.ds(at + 8 * j, 8), :]
-                    )
-                    fld[was, :] = new
-                    tiles.append(new)
-                split(r, jnp.concatenate(tiles, axis=0))
+                    fresh.append(jnp.concatenate(tiles, axis=0))
+                for g, new in enumerate(fresh):
+                    fld[pl.ds(back + SLAB * g, SLAB), :] = new
+                    split(pl.multiple_of(r + SLAB * g, SLAB), new)
 
             @pl.when(t < STEPS - 1)
             def _():
@@ -340,9 +331,6 @@
         return carry
 
     lax.fori_loop(0, STEPS, step, 0)
-    for n in range(4):
-        pair(n).wait_send()
-
     @pl.loop(0, 32)
     def _(y):
         for j in range(4):
@@ -355,6 +343,14 @@
 def body(
     pressure, pressure_prev, horiz_coef, vert_coef, traces, recv_cell, recv_owner, trace_counts
 ):
+    pairs = [(i, i ^ 1) for i in range(lax.axis_size("gy"))]
+
+    def swap(array):
+        return lax.ppermute(array, "gy", pairs)
+
+    blocks = [a.reshape(1024, 128) for a in (pressure, pressure_prev, horiz_coef, vert_coef)]
+    blocks += [swap(a) for a in (blocks[0], blocks[1], code(blocks[2]), code(blocks[3]))]
+
     samples = traces.shape[-1]
     columns, slots = recv_cell.shape[1:]
     per_step = samples // STEPS
@@ -369,24 +365,22 @@
     x, y, z = cell // 4096, (cell // 128) % 32, cell % 128
     live = jnp.arange(slots, dtype=jnp.int32)[None, :] < trace_counts[0][:, None]
     owner = jnp.where(live, recv_owner[0], -1)
-    code = jnp.stack([y, (x % 4) * 8 + x // 4, z, owner], axis=-1).astype(BF16)
+    tags = jnp.stack([y, (x % 4) * 8 + x // 4, z, owner], axis=-1).astype(BF16)
     packed = jnp.concatenate(
-        [amps, code, jnp.zeros((columns, slots, 28), BF16)], axis=-1
+        [amps, tags, jnp.zeros((columns, slots, 28), BF16)], axis=-1
     ).reshape(columns, 128)
     routed = lax.all_to_all(packed, ("gx", "gy"), split_axis=0, concat_axis=0, tiled=True)
     own = lax.all_gather(routed, "gz", axis=0, tiled=True)
-    pairs = [(i, i ^ 1) for i in range(lax.axis_size("gy"))]
-    other = lax.ppermute(own, "gy", pairs)
+    other = swap(own)
     low = lax.rem(lax.axis_index("gy"), 2) == 0
     table = jnp.stack([jnp.where(low, own, other), jnp.where(low, other, own)])
 
-    flat = [a.reshape(1024, 128) for a in (pressure, pressure_prev, horiz_coef, vert_coef)]
     vmem = pl.BlockSpec(memory_space=pltpu.VMEM)
     dma = pltpu.SemaphoreType.DMA
     outs = pl.pallas_call(
         kernel,
         out_shape=[jax.ShapeDtypeStruct((1024, 128), F32)] * 2,
-        in_specs=[vmem] * 5,
+        in_specs=[vmem] * 9,
         out_specs=[vmem] * 2,
         scratch_shapes=[
             pltpu.VMEM((2 * FIELD, 128), F32),
@@ -396,26 +390,24 @@
             pltpu.VMEM((NY * SLAB, 256), BF16),
             pltpu.VMEM((NY * SLAB, 512), BF16),
             pltpu.VMEM((1024, 128), F32),
-            pltpu.VMEM((1024, 128), BF16),
+            pltpu.VMEM((1024, 256), BF16),
             pltpu.VMEM((2, NY * 4, 128), F32),
             pltpu.VMEM((2, 2, NY * 4, 128), F32),
             pltpu.VMEM((NY * SLAB, 128), F32),
-            pltpu.VMEM((NCH, 16, 256), F32),
-            pltpu.VMEM((2, NCH, 16, 256), F32),
-            pltpu.VMEM((ROWS, 128), F32),
-            pltpu.VMEM((4, 1024, 128), F32),
-            pltpu.VMEM((256, 128), BF16),
-            pltpu.VMEM((2, 16, 256), BF16),
-            pltpu.VMEM((2, 32, 128), BF16),
+            pltpu.VMEM((NCH, 32, 128), F32),
+            pltpu.VMEM((2, NCH, 2, 32, 128), F32),
+            pltpu.VMEM((2, 1024, 128), F32),
+            pltpu.VMEM((256, 256), BF16),
+            pltpu.VMEM((NY * SLAB, 128), F32),
+            pltpu.VMEM((2, NY * SLAB, 128), F32),
             dma((2,)), dma((2, 2)),
             dma((2, NCH)), dma((2, 2, NCH)),
             dma((2, NCH)), dma((2, 2, NCH)),
-            dma((4,)), dma((4,)),
         ],
         compiler_params=pltpu.CompilerParams(
             collective_id=0, has_side_effects=True, vmem_limit_bytes=40 * 1024 * 1024
         ),
-    )(*flat, table)
+    )(*blocks, table)
     return tuple(o.reshape(32, 32, 128) for o in outs)
 
 

time: 404 us -> 264 us (0.65)
  Pallas kernels: 350 us -> 150 us
  starting transfers between devices: 0.26 us -> 31.7 us
  blocking collectives: 37.3 us -> 57 us
  waiting for transfers between devices: 6.76 us -> 15.1 us
    pallas_call x1, Pallas kernels: 350 us -> 150 us  [body(): pl.pallas_call(kernel, out_shape=[jax.ShapeDtypeStruct((1024, 128), F32)]...]
    all_gather x1, blocking collectives: 10.2 us -> 57 us  [body(): own = lax.all_gather(routed, 'gz', axis=0, tiled=True)]
    all_to_all x1 -> x0, blocking collectives: 27.1 us -> none  [body(): lax.all_to_all(packed, ('gx', 'gy'), split_axis=0, concat_axis=0, tiled=T...]
    ppermute x1 -> x5, starting transfers between devices: 0.26 us -> 16.1 us  [swap(): return lax.ppermute(array, 'gy', pairs)]
    all_to_all x0 -> x1, starting transfers between devices: none -> 15.6 us  [body(): lax.all_to_all(packed, ('gx', 'gy'), split_axis=0, concat_axis=0, tiled=T...]
    ppermute x1 -> x5, waiting for transfers between devices: 6.76 us -> 15 us  [swap(): return lax.ppermute(array, 'gy', pairs)]
  transfers between devices with their start and end apart: 1 -> 6, of which waited for: 1 -> 3; matrix products, arithmetic and copies ran while one was open for 0% -> 1% of each run, Pallas kernels for 0% -> 0%
where the time goes in v2:
time: 264 us
  Pallas kernels  150 us (57%)
  blocking collectives  57 us (22%)
  starting transfers between devices  31.7 us (12%)
  waiting for transfers between devices  15.1 us (6%)
  local copies, waits for them, and re-layouts  5.32 us (2%)
  other arithmetic  3.98 us (2%)
    pallas_call x1, Pallas kernels, body(): pl.pallas_call(kernel, out_shape=[jax.ShapeDtypeStruct((1024, 128), F32)]...  150 us
    all_gather x1, blocking collectives, body(): own = lax.all_gather(routed, 'gz', axis=0, tiled=True)  57 us
    ppermute x5, starting transfers between devices, swap(): return lax.ppermute(array, 'gy', pairs)  16.1 us
    all_to_all x1, starting transfers between devices, body(): lax.all_to_all(packed, ('gx', 'gy'), split_axis=0, concat_axis=0, tiled=T...  15.6 us
    ppermute x5, waiting for transfers between devices, swap(): return lax.ppermute(array, 'gy', pairs)  15 us
  transfers between devices with their start and end apart: 6, of which 3 were waited for; matrix products, arithmetic and copies ran while one was open for 1% of the time, Pallas kernels for 0%

profile of v2, /device:TPU:1, one launch (start us, length us, event | category | flops | bytes accessed | tf_op | source)
XLA Modules:
  0.0 263.7 jit_solution(16364400891324360241)
XLA Ops:
  0.6 0.0 copy-start
  0.6 0.0 copy-start.2
  0.7 0.7 copy-done
  1.4 0.2 fusion
  1.6 0.1 copy.21
  1.8 0.8 copy.22
  2.6 0.8 copy.26
  3.4 1.4 fusion.5
  4.8 0.0 copy-start.3
  4.8 0.5 concatenate.4
  5.4 0.0 copy-start.1
  5.4 0.7 all_to_all.11
  6.1 15.6 %all-to-all-start = ((bf16[64,1,128]{2,1,0:T(2,128)(2,1)}), bf16[64,1,128]{2,1,0:T(2,128)(2,1)S(1)}, u32[]{:S(2)}, u32[]{:S(2)}) async-start(bf16[64,1,128]{2,1,0:T(2,128)(2,1)} %all_to_all.11), calls=%async_computation | async-start | bytes 65536 | tf_op jit(solution)/shard_map/all_to_all | solution.py:372
  21.7 0.0 copy-done.2
  21.8 0.8 round-nearest-even_convert_fusion
  22.6 5.3 %collective-permute-start.3 = (s16[1024,128]{1,0:T(8,128)(2,1)}, s16[1024,128]{1,0:T(8,128)(2,1)S(1)}, u32[]{:S(2)}, u32[]{:S(2)}) collective-permute-start(s16[1024,128]{1,0:T(8,128)(2,1)} %round-nearest-even_convert_fusion), channel_id=1, source_target_pairs={{0,4},{4,0},{8,12},{12,8},{16,20},{20,16},{24,28},{28,24},{1,5},{5... | collective-permute-start | bytes 786440 | tf_op jit(solution)/shard_map/ppermute | solution.py:349
  27.9 0.0 copy-done.3
  27.9 0.1 collective-permute-start
  28.0 5.3 %collective-permute-start.1 = (f32[1024,128]{1,0:T(8,128)}, f32[1024,128]{1,0:T(8,128)S(1)}, u32[]{:S(2)}, u32[]{:S(2)}) collective-permute-start(f32[1024,128]{1,0:T(8,128)} %bitcast.30), channel_id=1, source_target_pairs={{0,4},{4,0},{8,12},{12,8},{16,20},{20,16},{24,28},{28,24},{1,5},{5... | collective-permute-start | bytes 1572872 | tf_op jit(solution)/shard_map/ppermute | solution.py:349
  33.2 0.1 all-to-all-done
  33.4 57.0 %all-gather = bf16[256,1,128]{2,0,1:T(8,128)(2,1)S(1)} all-gather(bf16[64,1,128]{2,0,1:T(8,128)(2,1)S(1)} %copy.28), channel_id=2, replica_groups=mesh['gx'=8,'gy'=8,'gz'=4] {'gz'}, dimensions={0}, use_global_device_ids=true | all-gather | bytes 81920 | tf_op jit(solution)/shard_map/all_gather | solution.py:373
  90.4 0.0 copy-start.4
  90.4 3.3 %collective-permute-start.4 = (bf16[256,128]{1,0:T(8,128)(2,1)S(1)}, bf16[256,128]{1,0:T(8,128)(2,1)}, u32[]{:S(2)}, u32[]{:S(2)}) collective-permute-start(bf16[256,128]{1,0:T(8,128)(2,1)S(1)} %bitcast.32), channel_id=1, source_target_pairs={{0,4},{4,0},{8,12},{12,8},{16,20},{20,16},{24,28},{28,24},{1,5},{5... | collective-permute-start | bytes 196616 | tf_op jit(solution)/shard_map/ppermute | solution.py:349
  93.7 0.0 copy-done.1
  93.7 0.8 round-nearest-even_convert_fusion.1
  94.6 2.1 collective-permute-start.2
  96.7 0.9 collective-permute-done.4
  97.6 0.9 select_bitcast_fusion.1
  98.5 0.0 collective-permute-done.3.ov_ref
  98.5 14.1 %collective-permute-done.2.oh_ref = s16[1024,128]{1,0:T(8,128)(2,1)} collective-permute-done((s16[1024,128]{1,0:T(8,128)(2,1)}, s16[1024,128]{1,0:T(8,128)(2,1)}, u32[]{:S(2)}, u32[]{:S(2)}) %collective-permute-start.2) | collective-permute-done | bytes 262176 | tf_op jit(solution)/shard_map/ppermute | solution.py:349
  112.5 0.0 collective-permute-done.op_ref
  112.6 0.0 collective-permute-done.1.oq_ref
  112.6 0.0 copy-done.4
  112.6 149.6 %shard_map.95 = (f32[1024,128]{1,0:T(8,128)S(1)}, f32[1024,128]{1,0:T(8,128)S(1)}) custom-call(f32[1024,128]{1,0:T(8,128)S(1)} %bitcast.29, f32[1024,128]{1,0:T(8,128)S(1)} %bitcast.31, f32[1024,128]{1,0:T(8,128)S(1)} %bitcast.24, f32[1024,128]{1,0:T(8,128)S(1)} %bitcast.25, f32[1024,128]{1,0:T(8,128)S(1)} %collective-permute-done.op_ref, ...), custom_call_target="tpu_custom_call" | custom-call | tf_op jit(solution)/shard_map/pallas_call | solution.py:380
  262.1 0.8 copy.31
  262.9 0.8 copy.32
  (5 shorter events, 0.0 us)
Async XLA Ops:
  0.6 0.8 copy-start
  0.6 21.1 %copy-start.2 = (f32[32,32,128]{2,1,0:T(8,128)S(1)}, f32[32,32,128]{2,1,0:T(8,128)}, u32[]{:S(2)}) copy-start(f32[32,32,128]{2,1,0:T(8,128)} %param.11) | copy-start | bytes 1572868
  4.8 23.0 %copy-start.3 = (f32[32,32,128]{2,1,0:T(8,128)S(1)}, f32[32,32,128]{2,1,0:T(8,128)}, u32[]{:S(2)}) copy-start(f32[32,32,128]{2,1,0:T(8,128)} %param.8) | copy-start | bytes 1572868
  5.4 88.3 %copy-start.1 = (f32[32,32,128]{2,1,0:T(8,128)S(1)}, f32[32,32,128]{2,1,0:T(8,128)}, u32[]{:S(2)}) copy-start(f32[32,32,128]{2,1,0:T(8,128)} %param.10) | copy-start | bytes 1572868
  6.1 27.3 %all-to-all-start = ((bf16[64,1,128]{2,1,0:T(2,128)(2,1)}), bf16[64,1,128]{2,1,0:T(2,128)(2,1)S(1)}, u32[]{:S(2)}, u32[]{:S(2)}) async-start(bf16[64,1,128]{2,1,0:T(2,128)(2,1)} %all_to_all.11), calls=%async_computation | async-start | bytes 65536 | tf_op jit(solution)/shard_map/all_to_all | solution.py:372
  22.6 75.9 %collective-permute-start.3 = (s16[1024,128]{1,0:T(8,128)(2,1)}, s16[1024,128]{1,0:T(8,128)(2,1)S(1)}, u32[]{:S(2)}, u32[]{:S(2)}) collective-permute-start(s16[1024,128]{1,0:T(8,128)(2,1)} %round-nearest-even_convert_fusion), channel_id=1, source_target_pairs={{0,4},{4,0},{8,12},{12,8},{16,20},{20,16},{24,28},{28,24},{1,5},{5... | collective-permute-start | bytes 786440 | tf_op jit(solution)/shard_map/ppermute | solution.py:349
  27.9 84.7 %collective-permute-start = (f32[1024,128]{1,0:T(8,128)S(1)}, f32[1024,128]{1,0:T(8,128)S(1)}, u32[]{:S(2)}, u32[]{:S(2)}) collective-permute-start(f32[1024,128]{1,0:T(8,128)S(1)} %bitcast.28), channel_id=1, source_target_pairs={{0,4},{4,0},{8,12},{12,8},{16,20},{20,16},{24,28},{28,24},{1,5},{5... | collective-permute-start | bytes 1572872 | tf_op jit(solution)/shard_map/ppermute | solution.py:349
  28.0 84.6 %collective-permute-start.1 = (f32[1024,128]{1,0:T(8,128)}, f32[1024,128]{1,0:T(8,128)S(1)}, u32[]{:S(2)}, u32[]{:S(2)}) collective-permute-start(f32[1024,128]{1,0:T(8,128)} %bitcast.30), channel_id=1, source_target_pairs={{0,4},{4,0},{8,12},{12,8},{16,20},{20,16},{24,28},{28,24},{1,5},{5... | collective-permute-start | bytes 1572872 | tf_op jit(solution)/shard_map/ppermute | solution.py:349
  90.4 22.2 %copy-start.4 = (f32[32,32,128]{2,1,0:T(8,128)S(1)}, f32[32,32,128]{2,1,0:T(8,128)}, u32[]{:S(2)}) copy-start(f32[32,32,128]{2,1,0:T(8,128)} %param.9) | copy-start | bytes 1572868
  90.4 7.2 %collective-permute-start.4 = (bf16[256,128]{1,0:T(8,128)(2,1)S(1)}, bf16[256,128]{1,0:T(8,128)(2,1)}, u32[]{:S(2)}, u32[]{:S(2)}) collective-permute-start(bf16[256,128]{1,0:T(8,128)(2,1)S(1)} %bitcast.32), channel_id=1, source_target_pairs={{0,4},{4,0},{8,12},{12,8},{16,20},{20,16},{24,28},{28,24},{1,5},{5... | collective-permute-start | bytes 196616 | tf_op jit(solution)/shard_map/ppermute | solution.py:349
  94.6 18.0 %collective-permute-start.2 = (s16[1024,128]{1,0:T(8,128)(2,1)}, s16[1024,128]{1,0:T(8,128)(2,1)}, u32[]{:S(2)}, u32[]{:S(2)}) collective-permute-start(s16[1024,128]{1,0:T(8,128)(2,1)} %round-nearest-even_convert_fusion.1), channel_id=1, source_target_pairs={{0,4},{4,0},{8,12},{12,8},{16,20},{20,16},{24,28},{28,24},{1,5},{5... | collective-permute-start | bytes 786440 | tf_op jit(solution)/shard_map/ppermute | solution.py:349

commit v3 on v2

--- a/solution.py
+++ b/solution.py
@@ -31,7 +31,7 @@
 
 
 def code(value):
-    return jnp.round((value - 0.115) * (32767.0 / 0.075)).astype(jnp.int16)
+    return jnp.round((value - 0.115) * (32767.0 / 0.075)).astype(jnp.int32).astype(jnp.int16)
 
 
 def decode(value):
@@ -43,13 +43,15 @@
 
 
 def kernel(
-    p_ref, q_ref, h_ref, v_ref, op_ref, oq_ref, oh_ref, ov_ref, f_ref, outp_ref, outq_ref,
-    fld, hc, vc, kc, hl, hot, zhot, wgt, xs, xh, hb, zs, zh, raw, band, lap, src,
-    ysend, yrecv, xsend, xrecv, zsend, zrecv,
+    p_ref, q_ref, h_ref, v_ref, f_ref, outp_ref, outq_ref,
+    fld, hc, vc, kc, hl, hot, zhot, wgt, xs, xh, hb, zs, zh, raw, coded, rawcoded, peak, rawpeak, table, band, lap, src,
+    ysend, yrecv, xsend, xrecv, zsend, zrecv, psend, precv, tsend, trecv,
 ):
     gx, gy, gz = lax.axis_index("gx"), lax.axis_index("gy"), lax.axis_index("gz")
     nx, ny, nz = lax.axis_size("gx"), lax.axis_size("gy"), lax.axis_size("gz")
     half = lax.rem(gy, 2)
+    partner = gy + 1 - 2 * half
+    flip = lax.rem(gy // 2, 2) * (NCH - 1)
     has = {
         ("x", 0): gx > 0, ("x", 1): gx < nx - 1,
         ("y", 0): gy > 1, ("y", 1): gy < ny - 2,
@@ -69,8 +71,14 @@
         clear(fld, par * FIELD + (NY + 4) * SLAB, 4 * SLAB)
     zh[...] = jnp.zeros_like(zh)
 
+    mates = [
+        (n, {"gy": gy if same else partner, "gz": lax.rem(gz + d, nz)})
+        for n, (same, d) in enumerate([(s, d) for s in (True, False) for d in range(nz)][1:])
+    ]
     barrier = pltpu.get_barrier_semaphore()
-    greet = jnp.int32(0)
+    for _, mate in mates:
+        pl.semaphore_signal(barrier, inc=1, device_id=mate, device_id_type=MESH)
+    greet = jnp.int32(len(mates))
     for key, ok in has.items():
 
         @pl.when(ok)
@@ -79,6 +87,51 @@
 
         greet = greet + ok.astype(jnp.int32)
     pl.semaphore_wait(barrier, greet)
+
+    def tell(n, mate, col, depth):
+        return pltpu.make_async_remote_copy(
+            src_ref=f_ref,
+            dst_ref=table.at[col, depth],
+            send_sem=tsend.at[n],
+            recv_sem=trecv.at[col, depth],
+            device_id=mate,
+            device_id_type=MESH,
+        )
+
+    for n, mate in mates:
+        tell(n, mate, half, gz).start()
+    table[half, gz] = f_ref[...]
+
+    def pair(n):
+        src_ref = coded.at[n] if n < 4 else peak
+        dst_ref = rawcoded.at[n] if n < 4 else rawpeak
+        return pltpu.make_async_remote_copy(
+            src_ref=src_ref,
+            dst_ref=dst_ref,
+            send_sem=psend.at[n],
+            recv_sem=precv.at[n],
+            device_id={"gy": partner},
+            device_id_type=MESH,
+        )
+
+    for n, ref in ((2, h_ref), (3, v_ref)):
+        coded[n] = code(ref[...])
+    for n, ref in ((0, p_ref), (1, q_ref)):
+
+        @pl.loop(0, 32)
+        def _(x):
+            rows = pl.ds(pl.multiple_of(x * 32, 32), 32)
+            value = ref[rows, :]
+            top = jnp.max(jnp.abs(value), axis=0, keepdims=True)
+            top = jnp.where(top > 0.0, top, 1.0)
+            peak[n, pl.ds(x, 1), :] = top
+            coded[n, rows, :] = jnp.round(value / top * 32767.0).astype(jnp.int32).astype(jnp.int16)
+
+    for n, (same, d) in enumerate([(s, d) for s in (True, False) for d in range(nz)][1:]):
+        col, depth = half if same else 1 - half, lax.rem(gz + d, nz)
+        tell(n, mates[n][1], col, depth).wait_recv()
+    for n in range(5):
+        pair(n).start()
 
     @pl.loop(0, NCH)
     def _(c):
@@ -90,7 +143,7 @@
     band[:, 128:256] = taps(jnp.where(m < 4, 128 + m - depth, depth + 8 - m)).astype(BF16)
 
     for col in range(2):
-        packed = f_ref[col]
+        packed = table[col].reshape(256, 128)
         for k in range(2):
             pick = iota((8, 128), 1) == 64 * k + 32 + iota((8, 128), 0)
             by_lane = lax.dot_general(
@@ -125,9 +178,37 @@
                 kc[pl.ds(put, 8), :] = 2.0 + COEF[0] * (2.0 * h + v)
 
     arrange((p_ref, q_ref, h_ref, v_ref), 32 * half)
-    raw[0] = decode(oh_ref[...])
-    raw[1] = decode(ov_ref[...])
-    arrange((op_ref, oq_ref, raw.at[0], raw.at[1]), 32 - 32 * half)
+    @pl.loop(0, STEPS // 2)
+    def _(u):
+        for col in range(2):
+            for k in range(2):
+                when = 64 * k + 2 * u + iota((128, 256), 1) // 128
+                spread = jnp.where(iota((128, 256), 0) == when, 1.0, 0.0).astype(BF16)
+                amp = jnp.dot(table[col].reshape(256, 128), spread, preferred_element_type=F32)
+                at = pl.ds(col * 512 + k * 256, 256)
+                wgt[at, 0:128] = (zhot[at, :] * amp[:, 0:128]).astype(BF16)
+                wgt[at, 128:256] = (zhot[at, :] * amp[:, 128:256]).astype(BF16)
+
+        @pl.loop(0, 2 * NCH)
+        def _(b):
+            rows = pl.ds(pl.multiple_of(b * 256, 256), 256)
+            col = pl.multiple_of((b // NCH) * 512, 512)
+            both = jnp.dot(hot[rows, :], wgt[pl.ds(col, 512), :], preferred_element_type=F32)
+            src[2 * u, rows, :] = both[:, 0:128]
+            src[2 * u + 1, rows, :] = both[:, 128:256]
+
+    for n in range(5):
+        pair(n).wait_recv()
+    for n in range(2):
+        raw[2 + n] = decode(rawcoded[2 + n])
+
+        @pl.loop(0, 32)
+        def _(x):
+            rows = pl.ds(pl.multiple_of(x * 32, 32), 32)
+            scale = rawpeak[n, pl.ds(x, 1), :] * (1.0 / 32767.0)
+            raw[n, rows, :] = rawcoded[n, rows, :].astype(jnp.int32).astype(F32) * scale
+
+    arrange([raw.at[n] for n in range(4)], 32 - 32 * half)
 
     sub, lane = iota((8, 128), 0), iota((8, 128), 1)
     group = lax.rem((lane + 4) // 8, 16)
@@ -227,7 +308,7 @@
 
     @pl.loop(0, NCH)
     def _(i):
-        c = jnp.where(i == 0, 0, jnp.where(i == 1, NCH - 1, i - 1))
+        c = jnp.where(i == 0, flip, jnp.where(i == 1, NCH - 1 - flip, i - 1))
 
         @pl.loop(0, CHUNK)
         def _(y):
@@ -240,30 +321,9 @@
         par = lax.rem(t, 2)
         old, now = (1 - par) * FIELD + 4 * SLAB, par * FIELD + 4 * SLAB
 
-        @pl.when(par == 0)
-        def _():
-            for col in range(2):
-                for k in range(2):
-                    when = 64 * k + t + iota((128, 256), 1) // 128
-                    spread = jnp.where(iota((128, 256), 0) == when, 1.0, 0.0).astype(BF16)
-                    amp = jnp.dot(f_ref[col], spread, preferred_element_type=F32)
-                    at = pl.ds(col * 512 + k * 256, 256)
-                    wgt[at, 0:128] = (zhot[at, :] * amp[:, 0:128]).astype(BF16)
-                    wgt[at, 128:256] = (zhot[at, :] * amp[:, 128:256]).astype(BF16)
-
-            @pl.loop(0, 2 * NCH)
-            def _(b):
-                rows = pl.ds(pl.multiple_of(b * 256, 256), 256)
-                col = pl.multiple_of((b // NCH) * 512, 512)
-                both = jnp.dot(
-                    hot[rows, :], wgt[pl.ds(col, 512), :], preferred_element_type=F32
-                )
-                src[0, rows, :] = both[:, 0:128]
-                src[1, rows, :] = both[:, 128:256]
-
         @pl.loop(0, NCH)
         def _(i):
-            c = jnp.where(i == 0, 0, jnp.where(i == 1, NCH - 1, i - 1))
+            c = jnp.where(i == 0, flip, jnp.where(i == 1, NCH - 1 - flip, i - 1))
             first = pl.multiple_of(c * ROWS, ROWS)
             for side in range(2):
 
@@ -314,7 +374,7 @@
                         rolled = pltpu.roll(got, turn, 1) if turn else got
                         depth = lap[here, :] + jnp.where(rim, rolled, 0.0)
                         tiles.append(
-                            (src[par, here, :] - fld[pl.ds(back + spot, 8), :])
+                            (src[t, here, :] - fld[pl.ds(back + spot, 8), :])
                             + kc[here, :] * mid[j]
                             + hc[here, :] * total
                             + vc[here, :] * depth
@@ -331,6 +391,10 @@
         return carry
 
     lax.fori_loop(0, STEPS, step, 0)
+    for n in range(5):
+        pair(n).wait_send()
+    for n, mate in mates:
+        tell(n, mate, half, gz).wait_send()
     @pl.loop(0, 32)
     def _(y):
         for j in range(4):
@@ -343,13 +407,7 @@
 def body(
     pressure, pressure_prev, horiz_coef, vert_coef, traces, recv_cell, recv_owner, trace_counts
 ):
-    pairs = [(i, i ^ 1) for i in range(lax.axis_size("gy"))]
-
-    def swap(array):
-        return lax.ppermute(array, "gy", pairs)
-
     blocks = [a.reshape(1024, 128) for a in (pressure, pressure_prev, horiz_coef, vert_coef)]
-    blocks += [swap(a) for a in (blocks[0], blocks[1], code(blocks[2]), code(blocks[3]))]
 
     samples = traces.shape[-1]
     columns, slots = recv_cell.shape[1:]
@@ -370,17 +428,13 @@
         [amps, tags, jnp.zeros((columns, slots, 28), BF16)], axis=-1
     ).reshape(columns, 128)
     routed = lax.all_to_all(packed, ("gx", "gy"), split_axis=0, concat_axis=0, tiled=True)
-    own = lax.all_gather(routed, "gz", axis=0, tiled=True)
-    other = swap(own)
-    low = lax.rem(lax.axis_index("gy"), 2) == 0
-    table = jnp.stack([jnp.where(low, own, other), jnp.where(low, other, own)])
 
     vmem = pl.BlockSpec(memory_space=pltpu.VMEM)
     dma = pltpu.SemaphoreType.DMA
     outs = pl.pallas_call(
         kernel,
         out_shape=[jax.ShapeDtypeStruct((1024, 128), F32)] * 2,
-        in_specs=[vmem] * 9,
+        in_specs=[vmem] * 5,
         out_specs=[vmem] * 2,
         scratch_shapes=[
             pltpu.VMEM((2 * FIELD, 128), F32),
@@ -396,18 +450,25 @@
             pltpu.VMEM((NY * SLAB, 128), F32),
             pltpu.VMEM((NCH, 32, 128), F32),
             pltpu.VMEM((2, NCH, 2, 32, 128), F32),
-            pltpu.VMEM((2, 1024, 128), F32),
+            pltpu.VMEM((4, 1024, 128), F32),
+            pltpu.VMEM((4, 1024, 128), jnp.int16),
+            pltpu.VMEM((4, 1024, 128), jnp.int16),
+            pltpu.VMEM((2, 32, 128), F32),
+            pltpu.VMEM((2, 32, 128), F32),
+            pltpu.VMEM((2, 4, 64, 128), BF16),
             pltpu.VMEM((256, 256), BF16),
             pltpu.VMEM((NY * SLAB, 128), F32),
-            pltpu.VMEM((2, NY * SLAB, 128), F32),
+            pltpu.VMEM((STEPS, NY * SLAB, 128), F32),
             dma((2,)), dma((2, 2)),
             dma((2, NCH)), dma((2, 2, NCH)),
             dma((2, NCH)), dma((2, 2, NCH)),
+            dma((5,)), dma((5,)),
+            dma((7,)), dma((2, 4)),
         ],
         compiler_params=pltpu.CompilerParams(
-            collective_id=0, has_side_effects=True, vmem_limit_bytes=40 * 1024 * 1024
+            collective_id=0, has_side_effects=True, vmem_limit_bytes=54 * 1024 * 1024
         ),
-    )(*blocks, table)
+    )(*blocks, routed)
     return tuple(o.reshape(32, 32, 128) for o in outs)
 
 

time: 264 us -> 219 us (0.83)
  Pallas kernels: 150 us -> 183 us
  starting transfers between devices: 31.7 us -> 0 us
  blocking collectives: 57 us -> 27.1 us
  waiting for transfers between devices: 15.1 us -> 0 us
  other arithmetic: 3.98 us -> 0.8 us
    all_gather x1 -> x0, blocking collectives: 57 us -> none  [body(): own = lax.all_gather(routed, 'gz', axis=0, tiled=True)]
    pallas_call x1, Pallas kernels: 150 us -> 183 us  [body(): pl.pallas_call(kernel, out_shape=[jax.ShapeDtypeStruct((1024, 128), F32)]...]
    all_to_all x0 -> x1, blocking collectives: none -> 27.1 us  [body(): lax.all_to_all(packed, ('gx', 'gy'), split_axis=0, concat_axis=0, tiled=T...]
    ppermute x5 -> x0, starting transfers between devices: 16.1 us -> none  [swap(): return lax.ppermute(array, 'gy', pairs)]
    all_to_all x1 -> x0, starting transfers between devices: 15.6 us -> none  [body(): lax.all_to_all(packed, ('gx', 'gy'), split_axis=0, concat_axis=0, tiled=T...]
    ppermute x5 -> x0, waiting for transfers between devices: 15 us -> none  [swap(): return lax.ppermute(array, 'gy', pairs)]
    unnamed x12 -> x13, local copies, waits for them, and re-layouts: 2.33 us -> 6.08 us
  transfers between devices with their start and end apart: 6 -> 0, of which waited for: 3 -> 0; matrix products, arithmetic and copies ran while one was open for 1% -> 0% of each run, Pallas kernels for 0% -> 0%
where the time goes in v3:
time: 219 us
  Pallas kernels  183 us (84%)
  blocking collectives  27.1 us (12%)
  local copies, waits for them, and re-layouts  7.09 us (3%)
    pallas_call x1, Pallas kernels, body(): pl.pallas_call(kernel, out_shape=[jax.ShapeDtypeStruct((1024, 128), F32)]...  183 us
    all_to_all x1, blocking collectives, body(): lax.all_to_all(packed, ('gx', 'gy'), split_axis=0, concat_axis=0, tiled=T...  27.1 us
    unnamed x13, local copies, waits for them, and re-layouts  6.08 us

profile of v3, /device:TPU:1, one launch (start us, length us, event | category | flops | bytes accessed | tf_op | source)
XLA Modules:
  0.0 218.5 jit_solution(10566543178026134988)
XLA Ops:
  0.6 0.0 copy-start
  0.7 0.7 copy-done
  1.4 0.2 fusion
  1.6 0.1 copy.28
  1.8 0.0 copy-start.2
  1.8 0.7 copy-done.2
  2.4 0.1 copy.29
  2.6 0.0 copy-start.3
  2.6 0.7 copy-done.3
  3.3 0.1 copy.33
  3.4 0.0 copy-start.4
  3.4 0.6 copy-done.4
  4.0 0.8 fusion.5
  4.9 0.5 concatenate.4
  5.4 0.1 all_to_all.10
  5.5 27.1 %all_to_all.12 = bf16[64,1,128]{2,1,0:T(2,128)(2,1)S(1)} all-to-all(bf16[64,1,128]{2,1,0:T(2,128)(2,1)S(1)} %all_to_all.10), channel_id=1, replica_groups=mesh['gx'=8,'gy'=8,'gz'=4] {'gx','gy'}, dimensions={0} | all-to-all | bytes 32768 | tf_op jit(solution)/shard_map/all_to_all | solution.py:430
  32.6 0.6 copy.37
  33.2 182.6 %shard_map.95 = (f32[1024,128]{1,0:T(8,128)}, f32[1024,128]{1,0:T(8,128)}) custom-call(f32[1024,128]{1,0:T(8,128)} %bitcast.20, f32[1024,128]{1,0:T(8,128)} %bitcast.21, f32[1024,128]{1,0:T(8,128)} %bitcast.22, f32[1024,128]{1,0:T(8,128)} %bitcast.23, bf16[64,128]{1,0:T(8,128)(2,1)} %bitcast.25), custom_call_target="tpu_custom_call" | custom-call | tf_op jit(solution)/shard_map/pallas_call | solution.py:434
  215.8 0.0 copy-start.1
  215.8 1.9 copy.40
  217.7 0.0 copy-done.1
  217.7 0.8 copy.41
  (3 shorter events, 0.0 us)
Async XLA Ops:
  0.6 0.8 copy-start
  1.8 0.7 copy-start.2
  2.6 0.7 copy-start.3
  3.4 0.7 copy-start.4
  215.8 1.9 copy-start.1

commit v4 on v3

--- a/solution.py
+++ b/solution.py
@@ -43,9 +43,9 @@
 
 
 def kernel(
-    p_ref, q_ref, h_ref, v_ref, f_ref, outp_ref, outq_ref,
-    fld, hc, vc, kc, hl, hot, zhot, wgt, xs, xh, hb, zs, zh, raw, coded, rawcoded, peak, rawpeak, table, band, lap, src,
-    ysend, yrecv, xsend, xrecv, zsend, zrecv, psend, precv, tsend, trecv,
+    p_ref, q_ref, h_ref, v_ref, rawcoded, rawpeak, f_ref, outp_ref, outq_ref,
+    fld, hc, vc, kc, hl, hot, zhot, wgt, xs, xh, hb, zs, zh, raw, table, band, lap, src,
+    ysend, yrecv, xsend, xrecv, zsend, zrecv, tsend, trecv,
 ):
     gx, gy, gz = lax.axis_index("gx"), lax.axis_index("gy"), lax.axis_index("gz")
     nx, ny, nz = lax.axis_size("gx"), lax.axis_size("gy"), lax.axis_size("gz")
@@ -102,36 +102,9 @@
         tell(n, mate, half, gz).start()
     table[half, gz] = f_ref[...]
 
-    def pair(n):
-        src_ref = coded.at[n] if n < 4 else peak
-        dst_ref = rawcoded.at[n] if n < 4 else rawpeak
-        return pltpu.make_async_remote_copy(
-            src_ref=src_ref,
-            dst_ref=dst_ref,
-            send_sem=psend.at[n],
-            recv_sem=precv.at[n],
-            device_id={"gy": partner},
-            device_id_type=MESH,
-        )
-
-    for n, ref in ((2, h_ref), (3, v_ref)):
-        coded[n] = code(ref[...])
-    for n, ref in ((0, p_ref), (1, q_ref)):
-
-        @pl.loop(0, 32)
-        def _(x):
-            rows = pl.ds(pl.multiple_of(x * 32, 32), 32)
-            value = ref[rows, :]
-            top = jnp.max(jnp.abs(value), axis=0, keepdims=True)
-            top = jnp.where(top > 0.0, top, 1.0)
-            peak[n, pl.ds(x, 1), :] = top
-            coded[n, rows, :] = jnp.round(value / top * 32767.0).astype(jnp.int32).astype(jnp.int16)
-
     for n, (same, d) in enumerate([(s, d) for s in (True, False) for d in range(nz)][1:]):
         col, depth = half if same else 1 - half, lax.rem(gz + d, nz)
         tell(n, mates[n][1], col, depth).wait_recv()
-    for n in range(5):
-        pair(n).start()
 
     @pl.loop(0, NCH)
     def _(c):
@@ -165,7 +138,7 @@
             )
 
     def arrange(refs, first):
-        @pl.loop(0, 32)
+        @pl.loop(0, 32, unroll=4)
         def _(y):
             for j in range(4):
                 take = pl.ds(j * 32 + y, 8, stride=128)
@@ -178,31 +151,29 @@
                 kc[pl.ds(put, 8), :] = 2.0 + COEF[0] * (2.0 * h + v)
 
     arrange((p_ref, q_ref, h_ref, v_ref), 32 * half)
-    @pl.loop(0, STEPS // 2)
-    def _(u):
-        for col in range(2):
-            for k in range(2):
-                when = 64 * k + 2 * u + iota((128, 256), 1) // 128
-                spread = jnp.where(iota((128, 256), 0) == when, 1.0, 0.0).astype(BF16)
-                amp = jnp.dot(table[col].reshape(256, 128), spread, preferred_element_type=F32)
-                at = pl.ds(col * 512 + k * 256, 256)
-                wgt[at, 0:128] = (zhot[at, :] * amp[:, 0:128]).astype(BF16)
-                wgt[at, 128:256] = (zhot[at, :] * amp[:, 128:256]).astype(BF16)
-
-        @pl.loop(0, 2 * NCH)
-        def _(b):
-            rows = pl.ds(pl.multiple_of(b * 256, 256), 256)
-            col = pl.multiple_of((b // NCH) * 512, 512)
-            both = jnp.dot(hot[rows, :], wgt[pl.ds(col, 512), :], preferred_element_type=F32)
-            src[2 * u, rows, :] = both[:, 0:128]
-            src[2 * u + 1, rows, :] = both[:, 128:256]
-
-    for n in range(5):
-        pair(n).wait_recv()
+    def sources(u, col):
+        for k in range(2):
+            when = 64 * k + 2 * u + iota((128, 256), 1) // 128
+            spread = jnp.where(iota((128, 256), 0) == when, 1.0, 0.0).astype(BF16)
+            amp = jnp.dot(table[col].reshape(256, 128), spread, preferred_element_type=F32)
+            at = pl.ds(pl.multiple_of(col * 512 + k * 256, 256), 256)
+            wgt[k * 256 : k * 256 + 256, 0:128] = (zhot[at, :] * amp[:, 0:128]).astype(BF16)
+            wgt[k * 256 : k * 256 + 256, 128:256] = (zhot[at, :] * amp[:, 128:256]).astype(BF16)
+        slot = 2 * lax.rem(u, 2)
+
+        rows = pl.ds(pl.multiple_of(col * 1024, 1024), 1024)
+        both = jnp.dot(hot[rows, :], wgt[...], preferred_element_type=F32)
+        src[slot, rows, :] = both[:, 0:128]
+        src[slot + 1, rows, :] = both[:, 128:256]
+
+    @pl.loop(0, 2)
+    def _(col):
+        sources(0, col)
+
     for n in range(2):
         raw[2 + n] = decode(rawcoded[2 + n])
 
-        @pl.loop(0, 32)
+        @pl.loop(0, 32, unroll=8)
         def _(x):
             rows = pl.ds(pl.multiple_of(x * 32, 32), 32)
             scale = rawpeak[n, pl.ds(x, 1), :] * (1.0 / 32767.0)
@@ -310,7 +281,7 @@
     def _(i):
         c = jnp.where(i == 0, flip, jnp.where(i == 1, NCH - 1 - flip, i - 1))
 
-        @pl.loop(0, CHUNK)
+        @pl.loop(0, CHUNK, unroll=4)
         def _(y):
             start = pl.multiple_of(c * ROWS + y * SLAB, SLAB)
             split(start, fld[pl.ds(start + 4 * SLAB, SLAB), :])
@@ -320,6 +291,10 @@
     def step(t, carry):
         par = lax.rem(t, 2)
         old, now = (1 - par) * FIELD + 4 * SLAB, par * FIELD + 4 * SLAB
+
+        @pl.when(t < STEPS - 2)
+        def _():
+            sources(t // 2 + 1, par)
 
         @pl.loop(0, NCH)
         def _(i):
@@ -374,7 +349,7 @@
                         rolled = pltpu.roll(got, turn, 1) if turn else got
                         depth = lap[here, :] + jnp.where(rim, rolled, 0.0)
                         tiles.append(
-                            (src[t, here, :] - fld[pl.ds(back + spot, 8), :])
+                            (src[lax.rem(t, 4), here, :] - fld[pl.ds(back + spot, 8), :])
                             + kc[here, :] * mid[j]
                             + hc[here, :] * total
                             + vc[here, :] * depth
@@ -391,11 +366,9 @@
         return carry
 
     lax.fori_loop(0, STEPS, step, 0)
-    for n in range(5):
-        pair(n).wait_send()
     for n, mate in mates:
         tell(n, mate, half, gz).wait_send()
-    @pl.loop(0, 32)
+    @pl.loop(0, 32, unroll=4)
     def _(y):
         for j in range(4):
             put = pl.ds(j * 32 + y, 8, stride=128)
@@ -407,6 +380,19 @@
 def body(
     pressure, pressure_prev, horiz_coef, vert_coef, traces, recv_cell, recv_owner, trace_counts
 ):
+    coded, peaks = [], []
+    for a in (pressure, pressure_prev):
+        top = jnp.max(jnp.abs(a), axis=1, keepdims=True)
+        top = jnp.where(top > 0.0, top, 1.0)
+        coded.append(jnp.round(a * (32767.0 / top)).astype(jnp.int32).astype(jnp.int16))
+        peaks.append(top[:, 0])
+    coded += [code(horiz_coef), code(vert_coef)]
+    coded, peaks = jnp.stack(coded).reshape(4, 1024, 128), jnp.stack(peaks)
+    coded, peaks, traces = lax.optimization_barrier((coded, peaks, traces))
+    pairs = [(i, i ^ 1) for i in range(lax.axis_size("gy"))]
+    other_peak = lax.ppermute(peaks, "gy", pairs)
+    other = lax.ppermute(coded, "gy", pairs)
+
     blocks = [a.reshape(1024, 128) for a in (pressure, pressure_prev, horiz_coef, vert_coef)]
 
     samples = traces.shape[-1]
@@ -434,7 +420,7 @@
     outs = pl.pallas_call(
         kernel,
         out_shape=[jax.ShapeDtypeStruct((1024, 128), F32)] * 2,
-        in_specs=[vmem] * 5,
+        in_specs=[vmem] * 7,
         out_specs=[vmem] * 2,
         scratch_shapes=[
             pltpu.VMEM((2 * FIELD, 128), F32),
@@ -444,31 +430,26 @@
             pltpu.VMEM((NY * SLAB, 256), BF16),
             pltpu.VMEM((NY * SLAB, 512), BF16),
             pltpu.VMEM((1024, 128), F32),
-            pltpu.VMEM((1024, 256), BF16),
+            pltpu.VMEM((512, 256), BF16),
             pltpu.VMEM((2, NY * 4, 128), F32),
             pltpu.VMEM((2, 2, NY * 4, 128), F32),
             pltpu.VMEM((NY * SLAB, 128), F32),
             pltpu.VMEM((NCH, 32, 128), F32),
             pltpu.VMEM((2, NCH, 2, 32, 128), F32),
             pltpu.VMEM((4, 1024, 128), F32),
-            pltpu.VMEM((4, 1024, 128), jnp.int16),
-            pltpu.VMEM((4, 1024, 128), jnp.int16),
-            pltpu.VMEM((2, 32, 128), F32),
-            pltpu.VMEM((2, 32, 128), F32),
             pltpu.VMEM((2, 4, 64, 128), BF16),
             pltpu.VMEM((256, 256), BF16),
             pltpu.VMEM((NY * SLAB, 128), F32),
-            pltpu.VMEM((STEPS, NY * SLAB, 128), F32),
+            pltpu.VMEM((4, NY * SLAB, 128), F32),
             dma((2,)), dma((2, 2)),
             dma((2, NCH)), dma((2, 2, NCH)),
             dma((2, NCH)), dma((2, 2, NCH)),
-            dma((5,)), dma((5,)),
             dma((7,)), dma((2, 4)),
         ],
         compiler_params=pltpu.CompilerParams(
-            collective_id=0, has_side_effects=True, vmem_limit_bytes=54 * 1024 * 1024
+            collective_id=0, has_side_effects=True, vmem_limit_bytes=40 * 1024 * 1024
         ),
-    )(*blocks, routed)
+    )(*blocks, other, other_peak, routed)
     return tuple(o.reshape(32, 32, 128) for o in outs)
 
 

time: 219 us -> 204 us (0.932)
  Pallas kernels: 183 us -> 154 us
  starting transfers between devices: 0 us -> 7.77 us
  blocking collectives: 27.1 us -> 31.6 us
  other arithmetic: 0.8 us -> 3.45 us
    pallas_call x1, Pallas kernels: 183 us -> 154 us  [body(): pl.pallas_call(kernel, out_shape=[jax.ShapeDtypeStruct((1024, 128), F32)]...]
    ppermute x0 -> x2, starting transfers between devices: none -> 7.77 us  [the longest x1 7.74 us: body(): other = lax.ppermute(coded, 'gy', pairs)]
    all_to_all x1, blocking collectives: 27.1 us -> 31.6 us  [body(): lax.all_to_all(packed, ('gx', 'gy'), split_axis=0, concat_axis=0, tiled=T...]
    unnamed x13 -> x19, local copies, waits for them, and re-layouts: 6.08 us -> 5.48 us
  transfers between devices with their start and end apart: 0 -> 2, of which waited for: 0 -> 0; matrix products, arithmetic and copies ran while one was open for 0% -> 1% of each run, Pallas kernels for 0% -> 0%
where the time goes in v4:
time: 204 us
  Pallas kernels  154 us (75%)
  blocking collectives  31.6 us (15%)
  starting transfers between devices  7.77 us (4%)
  local copies, waits for them, and re-layouts  6.49 us (3%)
  other arithmetic  3.45 us (2%)
    pallas_call x1, Pallas kernels, body(): pl.pallas_call(kernel, out_shape=[jax.ShapeDtypeStruct((1024, 128), F32)]...  154 us
    all_to_all x1, blocking collectives, body(): lax.all_to_all(packed, ('gx', 'gy'), split_axis=0, concat_axis=0, tiled=T...  31.6 us
    ppermute x1, starting transfers between devices, body(): other = lax.ppermute(coded, 'gy', pairs)  7.74 us
    unnamed x19, local copies, waits for them, and re-layouts  5.48 us
  transfers between devices with their start and end apart: 2, of which 0 were waited for; matrix products, arithmetic and copies ran while one was open for 1% of the time, Pallas kernels for 0%

profile of v4, /device:TPU:1, one launch (start us, length us, event | category | flops | bytes accessed | tf_op | source)
XLA Modules:
  0.0 204.0 jit_solution(6827655330678356535)
XLA Ops:
  0.6 0.0 copy-start
  0.6 0.0 copy-start.1
  0.7 0.0 copy-start.4
  0.7 1.2 abs_reduce_fusion
  1.9 0.0 copy-done.1
  1.9 0.1 abs_reduce_fusion.1
  2.0 0.0 copy-start.3
  2.0 0.0 copy-done.4
  2.0 0.1 convert_convert_fusion
  2.1 0.9 copy-done.3
  3.0 0.0 copy-start.2
  3.0 0.1 convert_convert_fusion.1
  3.1 0.9 copy-done.2
  4.1 0.1 convert_convert_fusion.2
  4.1 0.1 convert_convert_fusion.3
  4.2 1.0 pad_add_fusion
  5.3 7.7 %collective-permute-start = (s16[4,1024,128]{2,1,0:T(8,128)(2,1)}, s16[4,1024,128]{2,1,0:T(8,128)(2,1)S(1)}, u32[]{:S(2)}, u32[]{:S(2)}) collective-permute-start(s16[4,1024,128]{2,1,0:T(8,128)(2,1)} %pad_add_fusion), channel_id=1, source_target_pairs={{0,4},{4,0},{8,12},{12,8},{16,20},{20,16},{24,28},{28,24},{1,5},{5... | collective-permute-start | bytes 3145736 | tf_op jit(solution)/shard_map/ppermute | solution.py:394
  13.0 0.0 collective-permute-start.1
  13.0 0.0 copy-done
  13.0 0.2 convolution_convert_fusion
  13.3 0.1 copy.28
  13.4 0.0 copy-start.5
  13.4 0.7 copy-done.5
  14.1 0.1 copy.29
  14.2 0.0 copy-start.6
  14.2 0.7 copy-done.6
  14.9 0.1 copy.33
  15.0 0.0 copy-start.7
  15.0 0.6 copy-done.7
  15.7 0.8 fusion.4
  16.5 0.5 concatenate.5
  17.1 0.1 all_to_all.10
  17.2 31.6 %all_to_all.12 = bf16[64,1,128]{2,1,0:T(2,128)(2,1)S(1)} all-to-all(bf16[64,1,128]{2,1,0:T(2,128)(2,1)S(1)} %all_to_all.10), channel_id=1, replica_groups=mesh['gx'=8,'gy'=8,'gz'=4] {'gx','gy'}, dimensions={0} | all-to-all | bytes 32768 | tf_op jit(solution)/shard_map/all_to_all | solution.py:416
  48.8 0.0 collective-permute-done.1.rawpeak
  48.8 0.0 collective-permute-done.rawcoded
  48.8 153.6 %shard_map.95 = (f32[1024,128]{1,0:T(8,128)S(1)}, f32[1024,128]{1,0:T(8,128)S(1)}) custom-call(f32[1024,128]{1,0:T(8,128)S(1)} %bitcast.24, f32[1024,128]{1,0:T(8,128)S(1)} %bitcast.25, f32[1024,128]{1,0:T(8,128)S(1)} %bitcast.26, f32[1024,128]{1,0:T(8,128)S(1)} %bitcast.27, s16[4,1024,128]{2,1,0:T(8,128)(2,1)S(1)} %collective-permute-done.rawcoded, ...), custom_call_target="tpu_custom_call" | custom-call | tf_op jit(solution)/shard_map/pallas_call | solution.py:420
  202.4 0.8 copy.40
  203.2 0.8 copy.41
  (8 shorter events, 0.1 us)
Async XLA Ops:
  0.6 12.4 %copy-start = (bf16[1,64,2,128]{3,2,1,0:T(2,128)(2,1)S(1)}, bf16[1,64,2,128]{3,2,1,0:T(2,128)(2,1)}, u32[]{:S(2)}) copy-start(bf16[1,64,2,128]{3,2,1,0:T(2,128)(2,1)} %param.12) | copy-start | bytes 98308
  0.6 1.2 copy-start.1
  0.7 1.4 copy-start.4
  2.0 1.1 copy-start.3
  3.0 1.0 copy-start.2
  5.3 43.5 %collective-permute-start = (s16[4,1024,128]{2,1,0:T(8,128)(2,1)}, s16[4,1024,128]{2,1,0:T(8,128)(2,1)S(1)}, u32[]{:S(2)}, u32[]{:S(2)}) collective-permute-start(s16[4,1024,128]{2,1,0:T(8,128)(2,1)} %pad_add_fusion), channel_id=1, source_target_pairs={{0,4},{4,0},{8,12},{12,8},{16,20},{20,16},{24,28},{28,24},{1,5},{5... | collective-permute-start | bytes 3145736 | tf_op jit(solution)/shard_map/ppermute | solution.py:394
  13.0 35.8 %collective-permute-start.1 = (f32[2,32,128]{2,1,0:T(8,128)S(1)}, f32[2,32,128]{2,1,0:T(8,128)S(1)}, u32[]{:S(2)}, u32[]{:S(2)}) collective-permute-start(f32[2,32,128]{2,1,0:T(8,128)S(1)} %pad_maximum_fusion), channel_id=1, source_target_pairs={{0,4},{4,0},{8,12},{12,8},{16,20},{20,16},{24,28},{28,24},{1,5},{5... | collective-permute-start | bytes 98312 | tf_op jit(solution)/shard_map/ppermute | solution.py:393
  13.4 0.7 copy-start.5
  14.2 0.7 copy-start.6
  15.0 0.7 copy-start.7

commit v5 on v4

--- a/solution.py
+++ b/solution.py
@@ -102,10 +102,6 @@
         tell(n, mate, half, gz).start()
     table[half, gz] = f_ref[...]
 
-    for n, (same, d) in enumerate([(s, d) for s in (True, False) for d in range(nz)][1:]):
-        col, depth = half if same else 1 - half, lax.rem(gz + d, nz)
-        tell(n, mates[n][1], col, depth).wait_recv()
-
     @pl.loop(0, NCH)
     def _(c):
         clear(hb, pl.multiple_of(c * ROWS, ROWS), ROWS)
@@ -114,6 +110,142 @@
     band[:, 0:128] = taps(jnp.abs(depth - iota((256, 128), 1))).astype(BF16)
     m = lax.rem(iota((256, 128), 1), 8)
     band[:, 128:256] = taps(jnp.where(m < 4, 128 + m - depth, depth + 8 - m)).astype(BF16)
+
+    def arrange(refs, first):
+        @pl.loop(0, 32, unroll=4)
+        def _(y):
+            for j in range(4):
+                take = pl.ds(j * 32 + y, 8, stride=128)
+                put = pl.multiple_of((first + y) * SLAB + j * 8, 8)
+                fld[pl.ds(put + 4 * SLAB, 8), :] = refs[0][take, :]
+                fld[pl.ds(put + 4 * SLAB + FIELD, 8), :] = refs[1][take, :]
+                h, v = refs[2][take, :], refs[3][take, :]
+                hc[pl.ds(put, 8), :] = h
+                vc[pl.ds(put, 8), :] = v * (1.0 / SCALE)
+                kc[pl.ds(put, 8), :] = 2.0 + COEF[0] * (2.0 * h + v)
+
+    arrange((p_ref, q_ref, h_ref, v_ref), 32 * half)
+    for n in range(2):
+        raw[2 + n] = decode(rawcoded[2 + n])
+
+        @pl.loop(0, 32, unroll=8)
+        def _(x):
+            rows = pl.ds(pl.multiple_of(x * 32, 32), 32)
+            scale = rawpeak[n, pl.ds(x, 1), :] * (1.0 / 32767.0)
+            raw[n, rows, :] = rawcoded[n, rows, :].astype(jnp.int32).astype(F32) * scale
+
+    arrange([raw.at[n] for n in range(4)], 32 - 32 * half)
+
+    sub, lane = iota((8, 128), 0), iota((8, 128), 1)
+    group = lax.rem((lane + 4) // 8, 16)
+    rim = (lane < 4) | (lane >= 124)
+    lower = lax.rem(lane, 8) < 4
+
+    def y_copy(side, par):
+        src = par * FIELD + (4 if side == 0 else NY) * SLAB
+        dst = par * FIELD + (NY + 4 if side == 0 else 0) * SLAB
+        return pltpu.make_async_remote_copy(
+            src_ref=fld.at[pl.ds(pl.multiple_of(src, 128), 128)],
+            dst_ref=fld.at[pl.ds(pl.multiple_of(dst, 128), 128)],
+            send_sem=ysend.at[side],
+            recv_sem=yrecv.at[1 - side, par],
+            device_id=peer["y", side],
+            device_id_type=MESH,
+        )
+
+    def y_wait(side, par):
+        here = pl.ds(pl.multiple_of(par * FIELD + (0 if side == 0 else NY + 4) * SLAB, 128), 128)
+        pltpu.make_async_remote_copy(
+            src_ref=fld.at[here], dst_ref=fld.at[here], send_sem=ysend.at[side],
+            recv_sem=yrecv.at[side, par], device_id=peer["y", side], device_id_type=MESH,
+        ).wait_recv()
+
+    def x_copy(side, c, par, there):
+        rows = pl.ds(pl.multiple_of(c * CHUNK * 4, 64), CHUNK * 4)
+        return pltpu.make_async_remote_copy(
+            src_ref=xs.at[side, rows],
+            dst_ref=xh.at[par, there, rows],
+            send_sem=xsend.at[side, c],
+            recv_sem=xrecv.at[there, par, c],
+            device_id=peer["x", side],
+            device_id_type=MESH,
+        )
+
+    def z_copy(side, c, par, there):
+        return pltpu.make_async_remote_copy(
+            src_ref=zs.at[c],
+            dst_ref=zh.at[par, c, there],
+            send_sem=zsend.at[side, c],
+            recv_sem=zrecv.at[there, par, c],
+            device_id=peer["z", side],
+            device_id_type=MESH,
+        )
+
+    def settle(c):
+        for side in range(2):
+
+            @pl.when(has["x", side])
+            def _():
+                x_copy(side, c, 0, 1 - side).wait_send()
+
+            @pl.when(has["z", side])
+            def _():
+                z_copy(side, c, 0, 1 - side).wait_send()
+
+            @pl.when(has["y", side] & (c == (0 if side == 0 else NCH - 1)))
+            def _():
+                y_copy(side, 0).wait_send()
+
+    def send(c, par):
+        for side in range(2):
+
+            @pl.when(has["y", side] & (c == (0 if side == 0 else NCH - 1)))
+            def _():
+                y_copy(side, par).start()
+
+        first = par * FIELD + (4 + c * CHUNK) * SLAB
+        rows = pl.ds(pl.multiple_of(c * CHUNK * 4, 64), CHUNK * 4)
+        for side in range(2):
+            xs[side, rows, :] = fld[pl.ds(first + 7 * side, CHUNK * 4, stride=8), :]
+
+            @pl.when(has["x", side])
+            def _():
+                x_copy(side, c, par, 1 - side).start()
+
+        start = pl.multiple_of(c * ROWS, ROWS)
+        both = jnp.dot(hl[pl.ds(start, ROWS), :], band[...], preferred_element_type=F32)
+        lap[pl.ds(start, ROWS), :] = both[:, 0:128]
+        for n in range(4):
+            packed = both[128 * n : 128 * n + 8, 128:256]
+            for i in range(1, 16):
+                at = 128 * n + 8 * i
+                packed = jnp.where(group == i, both[at : at + 8, 128:256], packed)
+            zs[c, pl.ds(8 * n, 8), :] = packed
+        for side in range(2):
+
+            @pl.when(has["z", side])
+            def _():
+                z_copy(side, c, par, 1 - side).start()
+
+    def split(start, new):
+        high = new.astype(BF16)
+        hl[pl.ds(start, SLAB), 0:128] = high
+        hl[pl.ds(start, SLAB), 128:256] = (new - high.astype(F32)).astype(BF16)
+
+    @pl.loop(0, NCH)
+    def _(i):
+        c = jnp.where(i == 0, flip, jnp.where(i == 1, NCH - 1 - flip, i - 1))
+
+        @pl.loop(0, CHUNK, unroll=4)
+        def _(y):
+            start = pl.multiple_of(c * ROWS + y * SLAB, SLAB)
+            split(start, fld[pl.ds(start + 4 * SLAB, SLAB), :])
+
+        send(c, 0)
+
+    for n, (same, d) in enumerate([(s, d) for s in (True, False) for d in range(nz)][1:]):
+        col, depth = half if same else 1 - half, lax.rem(gz + d, nz)
+        tell(n, mates[n][1], col, depth).wait_recv()
 
     for col in range(2):
         packed = table[col].reshape(256, 128)
@@ -137,20 +269,6 @@
                 z == iota((256, 128), 1), 1.0, 0.0
             )
 
-    def arrange(refs, first):
-        @pl.loop(0, 32, unroll=4)
-        def _(y):
-            for j in range(4):
-                take = pl.ds(j * 32 + y, 8, stride=128)
-                put = pl.multiple_of((first + y) * SLAB + j * 8, 8)
-                fld[pl.ds(put + 4 * SLAB, 8), :] = refs[0][take, :]
-                fld[pl.ds(put + 4 * SLAB + FIELD, 8), :] = refs[1][take, :]
-                h, v = refs[2][take, :], refs[3][take, :]
-                hc[pl.ds(put, 8), :] = h
-                vc[pl.ds(put, 8), :] = v * (1.0 / SCALE)
-                kc[pl.ds(put, 8), :] = 2.0 + COEF[0] * (2.0 * h + v)
-
-    arrange((p_ref, q_ref, h_ref, v_ref), 32 * half)
     def sources(u, col):
         for k in range(2):
             when = 64 * k + 2 * u + iota((128, 256), 1) // 128
@@ -169,124 +287,6 @@
     @pl.loop(0, 2)
     def _(col):
         sources(0, col)
-
-    for n in range(2):
-        raw[2 + n] = decode(rawcoded[2 + n])
-
-        @pl.loop(0, 32, unroll=8)
-        def _(x):
-            rows = pl.ds(pl.multiple_of(x * 32, 32), 32)
-            scale = rawpeak[n, pl.ds(x, 1), :] * (1.0 / 32767.0)
-            raw[n, rows, :] = rawcoded[n, rows, :].astype(jnp.int32).astype(F32) * scale
-
-    arrange([raw.at[n] for n in range(4)], 32 - 32 * half)
-
-    sub, lane = iota((8, 128), 0), iota((8, 128), 1)
-    group = lax.rem((lane + 4) // 8, 16)
-    rim = (lane < 4) | (lane >= 124)
-    lower = lax.rem(lane, 8) < 4
-
-    def y_copy(side, par):
-        src = par * FIELD + (4 if side == 0 else NY) * SLAB
-        dst = par * FIELD + (NY + 4 if side == 0 else 0) * SLAB
-        return pltpu.make_async_remote_copy(
-            src_ref=fld.at[pl.ds(pl.multiple_of(src, 128), 128)],
-            dst_ref=fld.at[pl.ds(pl.multiple_of(dst, 128), 128)],
-            send_sem=ysend.at[side],
-            recv_sem=yrecv.at[1 - side, par],
-            device_id=peer["y", side],
-            device_id_type=MESH,
-        )
-
-    def y_wait(side, par):
-        here = pl.ds(pl.multiple_of(par * FIELD + (0 if side == 0 else NY + 4) * SLAB, 128), 128)
-        pltpu.make_async_remote_copy(
-            src_ref=fld.at[here], dst_ref=fld.at[here], send_sem=ysend.at[side],
-            recv_sem=yrecv.at[side, par], device_id=peer["y", side], device_id_type=MESH,
-        ).wait_recv()
-
-    def x_copy(side, c, par, there):
-        rows = pl.ds(pl.multiple_of(c * CHUNK * 4, 64), CHUNK * 4)
-        return pltpu.make_async_remote_copy(
-            src_ref=xs.at[side, rows],
-            dst_ref=xh.at[par, there, rows],
-            send_sem=xsend.at[side, c],
-            recv_sem=xrecv.at[there, par, c],
-            device_id=peer["x", side],
-            device_id_type=MESH,
-        )
-
-    def z_copy(side, c, par, there):
-        return pltpu.make_async_remote_copy(
-            src_ref=zs.at[c],
-            dst_ref=zh.at[par, c, there],
-            send_sem=zsend.at[side, c],
-            recv_sem=zrecv.at[there, par, c],
-            device_id=peer["z", side],
-            device_id_type=MESH,
-        )
-
-    def settle(c):
-        for side in range(2):
-
-            @pl.when(has["x", side])
-            def _():
-                x_copy(side, c, 0, 1 - side).wait_send()
-
-            @pl.when(has["z", side])
-            def _():
-                z_copy(side, c, 0, 1 - side).wait_send()
-
-            @pl.when(has["y", side] & (c == (0 if side == 0 else NCH - 1)))
-            def _():
-                y_copy(side, 0).wait_send()
-
-    def send(c, par):
-        for side in range(2):
-
-            @pl.when(has["y", side] & (c == (0 if side == 0 else NCH - 1)))
-            def _():
-                y_copy(side, par).start()
-
-        first = par * FIELD + (4 + c * CHUNK) * SLAB
-        rows = pl.ds(pl.multiple_of(c * CHUNK * 4, 64), CHUNK * 4)
-        for side in range(2):
-            xs[side, rows, :] = fld[pl.ds(first + 7 * side, CHUNK * 4, stride=8), :]
-
-            @pl.when(has["x", side])
-            def _():
-                x_copy(side, c, par, 1 - side).start()
-
-        start = pl.multiple_of(c * ROWS, ROWS)
-        both = jnp.dot(hl[pl.ds(start, ROWS), :], band[...], preferred_element_type=F32)
-        lap[pl.ds(start, ROWS), :] = both[:, 0:128]
-        for n in range(4):
-            packed = both[128 * n : 128 * n + 8, 128:256]
-            for i in range(1, 16):
-                at = 128 * n + 8 * i
-                packed = jnp.where(group == i, both[at : at + 8, 128:256], packed)
-            zs[c, pl.ds(8 * n, 8), :] = packed
-        for side in range(2):
-
-            @pl.when(has["z", side])
-            def _():
-                z_copy(side, c, par, 1 - side).start()
-
-    def split(start, new):
-        high = new.astype(BF16)
-        hl[pl.ds(start, SLAB), 0:128] = high
-        hl[pl.ds(start, SLAB), 128:256] = (new - high.astype(F32)).astype(BF16)
-
-    @pl.loop(0, NCH)
-    def _(i):
-        c = jnp.where(i == 0, flip, jnp.where(i == 1, NCH - 1 - flip, i - 1))
-
-        @pl.loop(0, CHUNK, unroll=4)
-        def _(y):
-            start = pl.multiple_of(c * ROWS + y * SLAB, SLAB)
-            split(start, fld[pl.ds(start + 4 * SLAB, SLAB), :])
-
-        send(c, 0)
 
     def step(t, carry):
         par = lax.rem(t, 2)

time: 204 us -> 199 us (0.975)
  Pallas kernels: 154 us -> 149 us
    pallas_call x1, Pallas kernels: 154 us -> 149 us  [body(): pl.pallas_call(kernel, out_shape=[jax.ShapeDtypeStruct((1024, 128), F32)]...]
where the time goes in v5:
time: 199 us
  Pallas kernels  149 us (75%)
  blocking collectives  31.6 us (16%)
  starting transfers between devices  7.77 us (4%)
  local copies, waits for them, and re-layouts  6.49 us (3%)
  other arithmetic  3.45 us (2%)
    pallas_call x1, Pallas kernels, body(): pl.pallas_call(kernel, out_shape=[jax.ShapeDtypeStruct((1024, 128), F32)]...  149 us
    all_to_all x1, blocking collectives, body(): lax.all_to_all(packed, ('gx', 'gy'), split_axis=0, concat_axis=0, tiled=T...  31.6 us
    ppermute x1, starting transfers between devices, body(): other = lax.ppermute(coded, 'gy', pairs)  7.74 us
    unnamed x19, local copies, waits for them, and re-layouts  5.48 us
  transfers between devices with their start and end apart: 2, of which 0 were waited for; matrix products, arithmetic and copies ran while one was open for 1% of the time, Pallas kernels for 0%

profile of v5, /device:TPU:1, one launch (start us, length us, event | category | flops | bytes accessed | tf_op | source)
XLA Modules:
  0.0 199.2 jit_solution(4522091284963303896)
XLA Ops:
  0.6 0.0 copy-start
  0.6 0.0 copy-start.1
  0.7 0.0 copy-start.4
  0.7 1.2 abs_reduce_fusion
  1.9 0.0 copy-done.1
  1.9 0.1 abs_reduce_fusion.1
  2.0 0.0 copy-start.3
  2.0 0.0 copy-done.4
  2.0 0.1 convert_convert_fusion
  2.1 0.9 copy-done.3
  3.0 0.0 copy-start.2
  3.0 0.1 convert_convert_fusion.1
  3.1 0.9 copy-done.2
  4.1 0.1 convert_convert_fusion.2
  4.1 0.1 convert_convert_fusion.3
  4.2 1.0 pad_add_fusion
  5.3 7.7 %collective-permute-start = (s16[4,1024,128]{2,1,0:T(8,128)(2,1)}, s16[4,1024,128]{2,1,0:T(8,128)(2,1)S(1)}, u32[]{:S(2)}, u32[]{:S(2)}) collective-permute-start(s16[4,1024,128]{2,1,0:T(8,128)(2,1)} %pad_add_fusion), channel_id=1, source_target_pairs={{0,4},{4,0},{8,12},{12,8},{16,20},{20,16},{24,28},{28,24},{1,5},{5... | collective-permute-start | bytes 3145736 | tf_op jit(solution)/shard_map/ppermute | solution.py:394
  13.0 0.0 collective-permute-start.1
  13.0 0.0 copy-done
  13.0 0.2 convolution_convert_fusion
  13.3 0.1 copy.28
  13.4 0.0 copy-start.5
  13.4 0.7 copy-done.5
  14.1 0.1 copy.29
  14.2 0.0 copy-start.6
  14.2 0.7 copy-done.6
  14.9 0.1 copy.33
  15.0 0.0 copy-start.7
  15.0 0.6 copy-done.7
  15.7 0.8 fusion.4
  16.5 0.5 concatenate.5
  17.1 0.1 all_to_all.10
  17.2 31.6 %all_to_all.12 = bf16[64,1,128]{2,1,0:T(2,128)(2,1)S(1)} all-to-all(bf16[64,1,128]{2,1,0:T(2,128)(2,1)S(1)} %all_to_all.10), channel_id=1, replica_groups=mesh['gx'=8,'gy'=8,'gz'=4] {'gx','gy'}, dimensions={0} | all-to-all | bytes 32768 | tf_op jit(solution)/shard_map/all_to_all | solution.py:416
  48.8 0.0 collective-permute-done.1.rawpeak
  48.8 0.0 collective-permute-done.rawcoded
  48.8 148.9 %shard_map.95 = (f32[1024,128]{1,0:T(8,128)S(1)}, f32[1024,128]{1,0:T(8,128)S(1)}) custom-call(f32[1024,128]{1,0:T(8,128)S(1)} %bitcast.24, f32[1024,128]{1,0:T(8,128)S(1)} %bitcast.25, f32[1024,128]{1,0:T(8,128)S(1)} %bitcast.26, f32[1024,128]{1,0:T(8,128)S(1)} %bitcast.27, s16[4,1024,128]{2,1,0:T(8,128)(2,1)S(1)} %collective-permute-done.rawcoded, ...), custom_call_target="tpu_custom_call" | custom-call | tf_op jit(solution)/shard_map/pallas_call | solution.py:420
  197.6 0.8 copy.40
  198.4 0.8 copy.41
  (8 shorter events, 0.1 us)
Async XLA Ops:
  0.6 12.4 %copy-start = (bf16[1,64,2,128]{3,2,1,0:T(2,128)(2,1)S(1)}, bf16[1,64,2,128]{3,2,1,0:T(2,128)(2,1)}, u32[]{:S(2)}) copy-start(bf16[1,64,2,128]{3,2,1,0:T(2,128)(2,1)} %param.12) | copy-start | bytes 98308
  0.6 1.2 copy-start.1
  0.7 1.4 copy-start.4
  2.0 1.1 copy-start.3
  3.0 1.0 copy-start.2
  5.3 43.5 %collective-permute-start = (s16[4,1024,128]{2,1,0:T(8,128)(2,1)}, s16[4,1024,128]{2,1,0:T(8,128)(2,1)S(1)}, u32[]{:S(2)}, u32[]{:S(2)}) collective-permute-start(s16[4,1024,128]{2,1,0:T(8,128)(2,1)} %pad_add_fusion), channel_id=1, source_target_pairs={{0,4},{4,0},{8,12},{12,8},{16,20},{20,16},{24,28},{28,24},{1,5},{5... | collective-permute-start | bytes 3145736 | tf_op jit(solution)/shard_map/ppermute | solution.py:394
  13.0 35.8 %collective-permute-start.1 = (f32[2,32,128]{2,1,0:T(8,128)S(1)}, f32[2,32,128]{2,1,0:T(8,128)S(1)}, u32[]{:S(2)}, u32[]{:S(2)}) collective-permute-start(f32[2,32,128]{2,1,0:T(8,128)S(1)} %pad_maximum_fusion), channel_id=1, source_target_pairs={{0,4},{4,0},{8,12},{12,8},{16,20},{20,16},{24,28},{28,24},{1,5},{5... | collective-permute-start | bytes 98312 | tf_op jit(solution)/shard_map/ppermute | solution.py:393
  13.4 0.7 copy-start.5
  14.2 0.7 copy-start.6
  15.0 0.7 copy-start.7
